TPU v7x, 32 devices: a whole 2x2x4 slice. The times are simulated.
32 devices in a mesh: node: 4 (over z), local: 8 (over y, x, core).
Axes of the slice: x: 2, y: 2, z: 4, core: 2. Of those that a mesh axis runs over, the one named last changes fastest.
Arguments:
- acts: bfloat16 [2048, 8192], P('local', 'node'), may hold values from -6 to 6
- w_rot: bfloat16 [8192, 8192], P('local', 'node'), may hold values from -0.75 to 0.75
- signs: int32 [8192], replicated, may hold values from -1 to 1, as said below
- upstream: bfloat16 [2048, 8192], P('local', 'node'), may hold values from -6 to 6
Outputs:
- outputs: bfloat16 [2048, 8192], P('local', 'node')
- input_grad: bfloat16 [2048, 8192], P('local', 'node')
- grad_rot: float32 [8192, 8192], P('local', 'node')
Inputs may be any that keep to these rules, and one draw needn't show every extreme that they name: `signs`: each entry is -1 or +1.
All inputs are finite; a program needn't handle non-finite values.
Results may differ from a plain program's by a relative error of at most 0.017.
Values may be sent and summed in bfloat16 or wider, within the bound.
A program may use at most 192 MiB of HBM per device.

v0:
```python
import jax
import jax.numpy as jnp
from jax import lax
from jax.sharding import PartitionSpec as P

HBLK = 128


def sylvester(order_count):
    row_index = lax.broadcasted_iota(jnp.int32, (order_count, order_count), 0)
    col_index = lax.broadcasted_iota(jnp.int32, (order_count, order_count), 1)
    common = jnp.bitwise_and(row_index, col_index)
    parity = jnp.zeros((order_count, order_count), jnp.int32)
    for bit_index in range(order_count.bit_length() - 1):
        parity = parity + jnp.bitwise_and(jnp.right_shift(common, bit_index), 1)
    return (1 - 2 * jnp.bitwise_and(parity, 1)).astype(jnp.float32)


def unrotate(shard_piece, sign_piece, hadamard_bf):
    row_count = shard_piece.shape[0]
    col_count = shard_piece.shape[1]
    blocks = shard_piece.reshape(row_count // HBLK, HBLK, col_count)
    mixed = jnp.einsum("ij,bjc->bic", hadamard_bf, blocks, preferred_element_type=jnp.float32)
    scaled = mixed * (sign_piece.astype(jnp.float32).reshape(row_count // HBLK, HBLK, 1) / HBLK)
    return scaled.reshape(row_count, col_count).astype(jnp.bfloat16)


def rotate(values, sign_piece, hadamard_bf):
    tok_count = values.shape[0]
    col_count = values.shape[1]
    signed = values * sign_piece.astype(jnp.bfloat16)[None, :]
    blocks = signed.reshape(tok_count, col_count // HBLK, HBLK)
    mixed = jnp.einsum("tbj,jk->tbk", blocks, hadamard_bf, preferred_element_type=jnp.float32)
    return (mixed / HBLK).reshape(tok_count, col_count).astype(jnp.bfloat16)


def local(acts, w_rot, signs, upstream):
    tok_count = acts.shape[0]
    col_count = acts.shape[1]
    row_share = w_rot.shape[0]
    hadamard_bf = sylvester(HBLK).astype(jnp.bfloat16)
    gathered = lax.all_gather(acts, "node", axis=1, tiled=True)
    rotated = rotate(gathered, signs, hadamard_bf)
    weight = unrotate(lax.all_gather(w_rot, "local", axis=0, tiled=True), signs, hadamard_bf)
    out_total = jnp.dot(gathered, weight, preferred_element_type=jnp.float32)
    term_piece = lax.dot_general(
        upstream, weight, (((1,), (1,)), ((), ())), preferred_element_type=jnp.float32
    )
    term_total = term_piece
    out_total, input_terms = (out_total, term_total)
    outputs = out_total.astype(jnp.bfloat16)
    input_grad = lax.psum_scatter(
        input_terms.astype(jnp.bfloat16), "node", scatter_dimension=1, tiled=True
    )
    local_count = lax.axis_size("local")
    owner_cols = lax.all_to_all(rotated, "local", split_axis=1, concat_axis=0, tiled=True)
    all_upper = lax.all_gather(upstream, "local", axis=0, tiled=True)
    owner_groups = owner_cols.reshape(local_count, tok_count, row_share)
    upper_groups = all_upper.reshape(local_count, tok_count, col_count)

    def add_group(group_index, grad_total):
        rot_rows = lax.dynamic_index_in_dim(owner_groups, group_index, 0, keepdims=False)
        up_rows = lax.dynamic_index_in_dim(upper_groups, group_index, 0, keepdims=False)
        term_piece = lax.dot_general(
            rot_rows, up_rows, (((0,), (0,)), ((), ())), preferred_element_type=jnp.float32
        )
        term_piece = lax.optimization_barrier(term_piece.astype(jnp.bfloat16))
        return grad_total + term_piece.astype(jnp.float32)

    grad_rot = lax.fori_loop(
        0, local_count, add_group, jnp.zeros((row_share, col_count), jnp.float32)
    )
    return (outputs, input_grad, grad_rot)


def solution(mesh):
    placed = (P("local", "node"), P("local", "node"), P(), P("local", "node"))
    return jax.shard_map(
        local,
        mesh=mesh,
        in_specs=placed,
        out_specs=(P("local", "node"), P("local", "node"), P("local", "node")),
        check_vma=False,
    )
```

profile of v0, /device:TPU:0, one launch (start us, length us, event | category | flops | bytes accessed | tf_op | source)
XLA Modules:
  0.0 498.1 jit_solution(3724060960105926793)
XLA Ops:
  7.2 0.7 all-gather.6.cloned.1.call-update
  7.9 0.7 all-gather.4.cloned.1.call-update
  9.4 0.8 convert_element_type.64
  10.2 0.8 multiply_bitcast_fusion.1
  10.9 82.1 %all-gather.6.cloned.1.call-done = bf16[256,8192]{1,0:T(8,128)(2,1)} async-done(((bf16[256,2048]{1,0:T(8,128)(2,1)}), bf16[256,8192]{1,0:T(8,128)(2,1)}) %all-gather.6.cloned.1.call-update) | async-done | bytes 4194320 | tf_op jit(solution)/shard_map/all_gather | solution.py:42
  93.1 5.5 %multiply_convert_fusion = bf16[256,64,128]{0,2,1:T(8,128)(2,1)} fusion(bf16[256,8192]{1,0:T(8,128)(2,1)} %all-gather.6.cloned.1.call-done, bf16[8192]{0:T(1024)(128)(2,1)S(1)} %convert_element_type.64), kind=kOutput, calls=%fused_computation.11 | convolution fusion | flops 543588352 | bytes 8404992 | tf_op jit(solution)/shard_map/tbj,jk->tbk/dot_general | solution.py:33
  98.6 6.6 %copy.9 = bf16[256,8,1024]{2,0,1:T(8,128)(2,1)} copy(bf16[256,8,1024]{0,2,1:T(8,128)(2,1)} %bitcast.47) | data formatting | bytes 8388608 | tf_op jit(solution)/shard_map/convert_element_type | solution.py:34
  105.2 4.7 all-to-all-start
  110.0 189.2 %all-gather.4.cloned.1.call-done = bf16[8192,2048]{1,0:T(8,128)(2,1)} async-done(((bf16[1024,2048]{1,0:T(8,128)(2,1)}), bf16[8192,2048]{1,0:T(8,128)(2,1)}) %all-gather.4.cloned.1.call-update) | async-done | bytes 33554448 | tf_op jit(solution)/shard_map/all_gather | solution.py:44
  299.2 23.4 %fusion.5 = bf16[64,128,2048]{2,1,0:T(8,128)(2,1)} fusion(f32[64,128]{1,0:T(8,128)S(1)} %multiply_bitcast_fusion.1, bf16[64,128,2048]{2,1,0:T(8,128)(2,1)} %bitcast.46), kind=kOutput, calls=%fused_computation.8 | convolution fusion | flops 4328947712 | bytes 67141632 | tf_op jit(solution)/shard_map/ij,bjc->bic/dot_general | solution.py:23
  322.7 18.6 %fusion.6 = bf16[256,8192]{0,1:T(8,128)(2,1)} fusion(bf16[8192,2048]{1,0:T(8,128)(2,1)} %bitcast.44, bf16[256,2048]{1,0:T(8,128)(2,1)S(1)} %copy-done), kind=kOutput, calls=%fused_computation.10 | convolution fusion | flops 8592031744 | bytes 38797312 | tf_op jit(solution)/shard_map/dot_general | solution.py:46
  341.4 14.2 %all-gather.8.cloned.1.call-done = bf16[2048,2048]{1,0:T(8,128)(2,1)} async-done(((bf16[256,2048]{1,0:T(8,128)(2,1)}), bf16[2048,2048]{1,0:T(8,128)(2,1)}) %all-gather.8.cloned.1.call-update) | async-done | bytes 8388624 | tf_op jit(solution)/shard_map/all_gather | solution.py:57
  355.6 115.9 %while.14 = (s32[]{:T(128)}, f32[1024,2048]{1,0:T(8,128)}, bf16[8,256,1024]{2,1,0:T(8,128)(2,1)}, bf16[8,256,2048]{2,1,0:T(8,128)(2,1)}, s32[]{:T(128)}, /*index=5*/s32[]{:T(128)}) while((s32[]{:T(128)}, f32[1024,2048]{1,0:T(8,128)}, bf16[8,256,1024]{2,1,0:T(8,128)(2,1)}, bf16[8,256,2048]{2,1,0:T(8,128)(2,1)}, s32[]{:T(128)}, ...), condition=%wide.region_2.3_spmd.clone, body=%wide.region_1.2_spmd.clone.sunk | while | flops 1082130432 | bytes 26739788 | solution.py:70
  355.6 4.6 convolution_convert_fusion.4
  360.2 7.7 %select_add_fusion.2 = f32[1024,2048]{1,0:T(8,128)} fusion(f32[1024,2048]{1,0:T(8,128)} %get-tuple-element.141, bf16[1024,2048]{1,0:T(8,128)(2,1)} %convolution_convert_fusion.4, pred[]{:T(512)S(6)} %compare.3), kind=kLoop, calls=%fused_computation.clone.1 | loop fusion | flops 6291456 | bytes 20971520 | tf_op jit(solution)/shard_map/while/body/eval_jaxpr/add | solution.py:68
  367.9 4.6 convolution_convert_fusion.4
  372.6 10.2 %select_add_fusion.2 = f32[1024,2048]{1,0:T(8,128)} fusion(f32[1024,2048]{1,0:T(8,128)} %get-tuple-element.141, bf16[1024,2048]{1,0:T(8,128)(2,1)} %convolution_convert_fusion.4, pred[]{:T(512)S(6)} %compare.3), kind=kLoop, calls=%fused_computation.clone.1 | loop fusion | flops 6291456 | bytes 20971520 | tf_op jit(solution)/shard_map/while/body/eval_jaxpr/add | solution.py:68
  382.7 4.6 convolution_convert_fusion.4
  387.4 10.1 %select_add_fusion.2 = f32[1024,2048]{1,0:T(8,128)} fusion(f32[1024,2048]{1,0:T(8,128)} %get-tuple-element.141, bf16[1024,2048]{1,0:T(8,128)(2,1)} %convolution_convert_fusion.4, pred[]{:T(512)S(6)} %compare.3), kind=kLoop, calls=%fused_computation.clone.1 | loop fusion | flops 6291456 | bytes 20971520 | tf_op jit(solution)/shard_map/while/body/eval_jaxpr/add | solution.py:68
  397.5 4.7 convolution_convert_fusion.4
  402.1 10.2 %select_add_fusion.2 = f32[1024,2048]{1,0:T(8,128)} fusion(f32[1024,2048]{1,0:T(8,128)} %get-tuple-element.141, bf16[1024,2048]{1,0:T(8,128)(2,1)} %convolution_convert_fusion.4, pred[]{:T(512)S(6)} %compare.3), kind=kLoop, calls=%fused_computation.clone.1 | loop fusion | flops 6291456 | bytes 20971520 | tf_op jit(solution)/shard_map/while/body/eval_jaxpr/add | solution.py:68
  412.3 4.6 convolution_convert_fusion.4
  417.0 10.2 %select_add_fusion.2 = f32[1024,2048]{1,0:T(8,128)} fusion(f32[1024,2048]{1,0:T(8,128)} %get-tuple-element.141, bf16[1024,2048]{1,0:T(8,128)(2,1)} %convolution_convert_fusion.4, pred[]{:T(512)S(6)} %compare.3), kind=kLoop, calls=%fused_computation.clone.1 | loop fusion | flops 6291456 | bytes 20971520 | tf_op jit(solution)/shard_map/while/body/eval_jaxpr/add | solution.py:68
  427.2 4.6 convolution_convert_fusion.4
  431.8 10.2 %select_add_fusion.2 = f32[1024,2048]{1,0:T(8,128)} fusion(f32[1024,2048]{1,0:T(8,128)} %get-tuple-element.141, bf16[1024,2048]{1,0:T(8,128)(2,1)} %convolution_convert_fusion.4, pred[]{:T(512)S(6)} %compare.3), kind=kLoop, calls=%fused_computation.clone.1 | loop fusion | flops 6291456 | bytes 20971520 | tf_op jit(solution)/shard_map/while/body/eval_jaxpr/add | solution.py:68
  442.0 4.6 convolution_convert_fusion.4
  446.6 10.1 %select_add_fusion.2 = f32[1024,2048]{1,0:T(8,128)} fusion(f32[1024,2048]{1,0:T(8,128)} %get-tuple-element.141, bf16[1024,2048]{1,0:T(8,128)(2,1)} %convolution_convert_fusion.4, pred[]{:T(512)S(6)} %compare.3), kind=kLoop, calls=%fused_computation.clone.1 | loop fusion | flops 6291456 | bytes 20971520 | tf_op jit(solution)/shard_map/while/body/eval_jaxpr/add | solution.py:68
  456.8 4.6 convolution_convert_fusion.4
  461.4 10.1 %select_add_fusion.2 = f32[1024,2048]{1,0:T(8,128)} fusion(f32[1024,2048]{1,0:T(8,128)} %get-tuple-element.141, bf16[1024,2048]{1,0:T(8,128)(2,1)} %convolution_convert_fusion.4, pred[]{:T(512)S(6)} %compare.3), kind=kLoop, calls=%fused_computation.clone.1 | loop fusion | flops 6291456 | bytes 20971520 | tf_op jit(solution)/shard_map/while/body/eval_jaxpr/add | solution.py:68
  471.5 16.3 %fusion.12 = bf16[256,2048]{0,1:T(8,128)(2,1)S(1)} fusion(bf16[8192,2048]{1,0:T(8,128)(2,1)} %bitcast.45, bf16[256,8192]{1,0:T(8,128)(2,1)} %all-gather.6.cloned.1.call-done), kind=kOutput, calls=%fused_computation.17 | convolution fusion | flops 8590458880 | bytes 38797312 | tf_op jit(solution)/shard_map/dot_general | solution.py:45
  487.8 1.4 copy.10
  489.3 2.3 copy.11
  (11 shorter events, 0.9 us)
Async XLA Ops:
  7.2 85.9 %all-gather.6.cloned.1.call-start = ((), (), s32[]{:S(2)}) async-start(), calls=%async_computation.3 | async-start | bytes 5242880 | tf_op jit(solution)/shard_map/all_gather | solution.py:42
  7.9 291.3 %all-gather.4.cloned.1.call-start = ((), (), s32[]{:S(2)}) async-start(), calls=%async_computation.2 | async-start | bytes 37748736 | tf_op jit(solution)/shard_map/all_gather | solution.py:44
  8.6 346.9 %all-gather.8.cloned.1.call-start = ((), (), s32[]{:S(2)}) async-start(), calls=%async_computation.5 | async-start | bytes 9437184 | tf_op jit(solution)/shard_map/all_gather | solution.py:57
  105.2 236.2 %all-to-all-start = ((bf16[256,8,1024]{2,0,1:T(8,128)(2,1)}), bf16[256,8,1024]{2,0,1:T(8,128)(2,1)}, u32[]{:S(2)}, u32[]{:S(2)}) async-start(bf16[256,8,1024]{2,0,1:T(8,128)(2,1)} %copy.9), calls=%async_computation.1 | async-start | bytes 8388608 | tf_op jit(solution)/shard_map/all_to_all | solution.py:56
  109.9 379.3 %reduce-scatter.2.cloned.1.call-start = ((), (), s32[]{:S(2)}) async-start(), calls=%async_computation.4 | async-start | bytes 5242880 | tf_op jit(solution)/shard_map/reduce_scatter | solution.py:52
  299.2 23.4 %copy-start = (bf16[256,2048]{1,0:T(8,128)(2,1)S(1)}, bf16[256,2048]{1,0:T(8,128)(2,1)}, u32[]{:S(2)}) copy-start(bf16[256,2048]{1,0:T(8,128)(2,1)} %param.9) | copy-start | bytes 3145732
Sparse Core Ops, SparseCore 0:
  9.6 83.4 all-gather.5
  94.9 204.2 all-gather.3
  301.1 54.3 all-gather.7
  357.7 76.7 reduce-scatter.1
where the time goes:
time: 499 us; the launch traced here: 498 us
  waiting for transfers between devices  288 us (58%)
  matrix products  101 us (20%)
  other arithmetic  80.3 us (16%)
  between operations  13.8 us (3%)
  local copies, waits for them, and re-layouts  10.3 us (2%)
    all_gather x1, waiting for transfers between devices, local(): lax.all_gather(w_rot, 'local', axis=0, tiled=True)  189 us
    all_gather x1, waiting for transfers between devices, local(): gathered = lax.all_gather(acts, 'node', axis=1, tiled=True)  82.1 us
    add x8, other arithmetic, add_group(): return grad_total + term_piece.astype(jnp.float32)  78.8 us
    dot_general x8, matrix products, add_group(): lax.dot_general(rot_rows, up_rows, (((0,), (0,)), ((), ())), preferred_el...  37.1 us
    dot_general x1, matrix products, unrotate(): jnp.einsum('ij,bjc->bic', hadamard_bf, blocks, preferred_element_type=jnp...  23.4 us
    dot_general x1, matrix products, local(): lax.dot_general(upstream, weight, (((1,), (1,)), ((), ())), preferred_ele...  18.6 us
    dot_general x1, matrix products, local(): out_total = jnp.dot(gathered, weight, preferred_element_type=jnp.float32)  16.3 us
    all_gather x1, waiting for transfers between devices, local(): all_upper = lax.all_gather(upstream, 'local', axis=0, tiled=True)  14.2 us
  transfers between devices with their start and end apart: 5, of which 3 were waited for; matrix products, arithmetic and copies ran while one was open for 38% of the time, Pallas kernels for 0%

commit v1 on v0

v1 whole, which is shorter than its diff:
```python
import jax
import jax.numpy as jnp
from jax import lax
from jax.sharding import PartitionSpec as P

HBLK = 128


def sylvester(order_count):
    row_index = lax.broadcasted_iota(jnp.int32, (order_count, order_count), 0)
    col_index = lax.broadcasted_iota(jnp.int32, (order_count, order_count), 1)
    common = jnp.bitwise_and(row_index, col_index)
    parity = jnp.zeros((order_count, order_count), jnp.int32)
    for bit_index in range(order_count.bit_length() - 1):
        parity = parity + jnp.bitwise_and(jnp.right_shift(common, bit_index), 1)
    return (1 - 2 * jnp.bitwise_and(parity, 1)).astype(jnp.float32)


def local(acts, w_rot, signs, upstream):
    rows, cols = w_rot.shape
    blocks = rows // HBLK
    had = sylvester(HBLK)
    own_signs = lax.dynamic_slice_in_dim(signs, lax.axis_index("local") * rows, rows)
    own_signs = own_signs.astype(jnp.float32).reshape(blocks, HBLK)
    up_all = lax.all_gather(upstream, "local", axis=0, tiled=True)
    feats = lax.all_gather(acts, "node", axis=1, tiled=True)
    own = lax.all_to_all(feats, "local", split_axis=1, concat_axis=0, tiled=True)

    left = (own_signs[:, :, None] * had).astype(jnp.bfloat16)
    mixed = jnp.einsum(
        "bij,bjc->bic", left, w_rot.reshape(blocks, HBLK, cols), preferred_element_type=jnp.float32
    )
    weight = (mixed / HBLK).astype(jnp.bfloat16).reshape(rows, cols)

    terms = lax.dot_general(
        up_all, weight, (((1,), (1,)), ((), ())), preferred_element_type=jnp.float32
    ).astype(jnp.bfloat16)
    terms = lax.all_to_all(terms, "local", split_axis=0, concat_axis=1, tiled=True)
    input_grad = lax.psum_scatter(terms, "node", scatter_dimension=1, tiled=True)

    partial = jnp.dot(own, weight, preferred_element_type=jnp.float32).astype(jnp.bfloat16)
    outputs = lax.psum_scatter(partial, "local", scatter_dimension=0, tiled=True)

    right = (own_signs[:, :, None] * had).astype(jnp.bfloat16)
    rotated = jnp.einsum(
        "tbj,bjk->tbk", own.reshape(-1, blocks, HBLK), right, preferred_element_type=jnp.float32
    )
    rotated = (rotated / HBLK).astype(jnp.bfloat16).reshape(-1, rows)
    grad_rot = lax.dot_general(
        rotated, up_all, (((0,), (0,)), ((), ())), preferred_element_type=jnp.float32
    )
    return outputs, input_grad, grad_rot


def solution(mesh):
    spec = P("local", "node")
    return jax.shard_map(
        local, mesh=mesh, in_specs=(spec, spec, P(), spec), out_specs=(spec, spec, spec), check_vma=False
    )
```

time: 499 us -> 378 us (0.76)
  other arithmetic: 80.3 us -> 0.76 us
  blocking collectives: 0 us -> 74.8 us
  waiting for transfers between devices: 288 us -> 216 us
  matrix products: 101 us -> 45.3 us
  local copies, waits for them, and re-layouts: 10.3 us -> 22.1 us
    all_gather x3 -> x2, waiting for transfers between devices: 286 us -> 83.4 us  [the longest x1 83.4 us: local(): feats = lax.all_gather(acts, 'node', axis=1, tiled=True)]
    add x8 -> x0, other arithmetic: 78.8 us -> none  [add_group(): return grad_total + term_piece.astype(jnp.float32)]
    all_to_all x0 -> x1, blocking collectives: none -> 74.8 us  [local(): lax.all_to_all(terms, 'local', split_axis=0, concat_axis=1, tiled=True)]
    reduce_scatter x1 -> x2, waiting for transfers between devices: 0.01 us -> 72 us  [the longest x1 72 us: local(): lax.psum_scatter(terms, 'node', scatter_dimension=1, tiled=True)]
    all_to_all x1, waiting for transfers between devices: 0.01 us -> 60 us  [local(): lax.all_to_all(feats, 'local', split_axis=1, concat_axis=0, tiled=True)]
    dot_general x12 -> x5, matrix products: 101 us -> 45.3 us  [the longest x1 14.1 us: local(): jnp.dot(own, weight, preferred_element_type=jnp.float32)]
    all_to_all x0 -> x3, local copies, waits for them, and re-layouts: none -> 13.2 us  [the longest x2 6.74 us: local(): lax.all_to_all(terms, 'local', split_axis=0, concat_axis=1, tiled=True)]
    convert_element_type x1 -> x0, local copies, waits for them, and re-layouts: 6.64 us -> none  [rotate(): return (mixed / HBLK).reshape(tok_count, col_count).astype(jnp.bfloat16)]
  transfers between devices with their start and end apart: 5 -> 5, of which waited for: 3 -> 3; matrix products, arithmetic and copies ran while one was open for 38% -> 17% of each run, Pallas kernels for 0% -> 0%
where the time goes in v1:
time: 378 us
  waiting for transfers between devices  216 us (57%)
  blocking collectives  74.8 us (20%)
  matrix products  45.3 us (12%)
  local copies, waits for them, and re-layouts  22.1 us (6%)
  between operations  13.8 us (4%)
  starting transfers between devices  4.74 us (1%)
    all_gather x1, waiting for transfers between devices, local(): feats = lax.all_gather(acts, 'node', axis=1, tiled=True)  83.4 us
    all_to_all x1, blocking collectives, local(): lax.all_to_all(terms, 'local', split_axis=0, concat_axis=1, tiled=True)  74.8 us
    reduce_scatter x1, waiting for transfers between devices, local(): lax.psum_scatter(terms, 'node', scatter_dimension=1, tiled=True)  72 us
    all_to_all x1, waiting for transfers between devices, local(): lax.all_to_all(feats, 'local', split_axis=1, concat_axis=0, tiled=True)  60 us
    dot_general x1, matrix products, local(): jnp.dot(own, weight, preferred_element_type=jnp.float32)  14.1 us
    dot_general x1, matrix products, local(): lax.dot_general(up_all, weight, (((1,), (1,)), ((), ())), preferred_eleme...  13 us
    dot_general x1, matrix products, local(): lax.dot_general(rotated, up_all, (((0,), (0,)), ((), ())), preferred_elem...  11 us
    unnamed x7, local copies, waits for them, and re-layouts  8.85 us
  transfers between devices with their start and end apart: 5, of which 3 were waited for; matrix products, arithmetic and copies ran while one was open for 17% of the time, Pallas kernels for 0%

profile of v1, /device:TPU:0, one launch (start us, length us, event | category | flops | bytes accessed | tf_op | source)
XLA Modules:
  0.0 377.6 jit_solution(4200469188900581591)
XLA Ops:
  7.2 0.0 all-gather.3.cloned.1.call-start
  7.2 2.3 copy.22
  9.5 0.0 all-gather.3.cloned.1.call-update
  9.5 0.0 all-gather.5.cloned.1.call-start
  9.5 0.7 all-gather.5.cloned.1.call-update
  10.3 83.4 %all-gather.3.cloned.1.call-done = bf16[256,8192]{0,1:T(8,128)(2,1)} async-done(((bf16[256,2048]{0,1:T(8,128)(2,1)}), bf16[256,8192]{0,1:T(8,128)(2,1)}) %all-gather.3.cloned.1.call-update) | async-done | bytes 4194320 | tf_op jit(solution)/shard_map/all_gather | solution.py:26
  93.6 4.6 %all-to-all-start = ((bf16[256,8,1024]{0,2,1:T(8,128)(2,1)}), bf16[256,8,1024]{0,2,1:T(8,128)(2,1)}, u32[]{:S(2)}, u32[]{:S(2)}) async-start(bf16[256,8,1024]{0,2,1:T(8,128)(2,1)} %bitcast.35), calls=%async_computation | async-start | bytes 8388608 | tf_op jit(solution)/shard_map/all_to_all | solution.py:27
  98.2 0.0 reduce-scatter.3.cloned.1.call-start
  98.3 0.7 convert_bitcast_fusion.1
  99.0 0.1 subtract_convert_fusion
  99.0 5.8 %multiply_convert_fusion.1 = bf16[8,128,2048]{2,1,0:T(8,128)(2,1)} fusion(bf16[8,128,2048]{2,1,0:T(8,128)(2,1)} %bitcast.37, f32[128,128]{0,1:T(8,128)S(1)} %subtract_convert_fusion, f32[8,128]{1,0:T(8,128)S(1)} %convert_bitcast_fusion.1), kind=kOutput, calls=%fused_computation.2 | convolution fusion | flops 541327360 | bytes 8458240 | tf_op jit(solution)/shard_map/bij,bjc->bic/dot_general | solution.py:30
  104.8 60.0 %all-to-all-done = bf16[256,8,1024]{0,2,1:T(8,128)(2,1)} async-done(((bf16[256,8,1024]{0,2,1:T(8,128)(2,1)}), bf16[256,8,1024]{0,2,1:T(8,128)(2,1)}, u32[]{:S(2)}, u32[]{:S(2)}) %all-to-all-start) | async-done | bytes 4194336 | tf_op jit(solution)/shard_map/all_to_all | solution.py:27
  164.9 6.5 %copy.23 = bf16[8,256,1024]{2,1,0:T(8,128)(2,1)} copy(bf16[8,256,1024]{1,2,0:T(8,128)(2,1)} %bitcast.4) | data formatting | bytes 8388608 | tf_op jit(solution)/shard_map/all_to_all | solution.py:27
  171.3 14.1 %convert_bitcast_fusion = bf16[2048,2048]{0,1:T(8,128)(2,1)} fusion(bf16[1024,2048]{1,0:T(8,128)(2,1)} %bitcast.38, bf16[2048,1024]{1,0:T(8,128)(2,1)} %bitcast.30), kind=kOutput, calls=%fused_computation.1 | convolution fusion | flops 8594128896 | bytes 16777216 | tf_op jit(solution)/shard_map/dot_general | solution.py:41
  185.4 0.0 reduce-scatter.3.cloned.1.call-update
  185.4 0.0 reduce-scatter.5.cloned.1.call-start
  185.5 0.0 all-gather.5.cloned.1.call-done
  185.5 13.0 %convolution_convert_fusion = bf16[1024,2048]{1,0:T(8,128)(2,1)S(1)} fusion(bf16[1024,2048]{1,0:T(8,128)(2,1)} %bitcast.39, bf16[2048,2048]{1,0:T(8,128)(2,1)} %all-gather.5.cloned.1.call-done), kind=kOutput, calls=%fused_computation.5 | convolution fusion | flops 8592031744 | bytes 16777216 | tf_op jit(solution)/shard_map/dot_general | solution.py:35
  198.5 0.3 copy.35
  198.8 74.8 %all_to_all.38 = bf16[8,256,1024]{1,2,0:T(8,128)(2,1)} all-to-all(bf16[8,256,1024]{1,2,0:T(8,128)(2,1)S(1)} %bitcast.32), channel_id=1, replica_groups=mesh['node'=4,'local'=8] {'local'}, dimensions={0} | all-to-all | bytes 8388608 | tf_op jit(solution)/shard_map/all_to_all | solution.py:38
  273.7 6.5 %copy.25 = bf16[256,8192]{1,0:T(8,128)(2,1)} copy(bf16[256,8192]{0,1:T(8,128)(2,1)} %bitcast.33) | data formatting | bytes 8388608 | tf_op jit(solution)/shard_map/all_to_all | solution.py:38
  280.1 0.0 reduce-scatter.5.cloned.1.call-update
  280.1 0.0 slice-start
  280.2 3.5 copy.31
  283.6 0.0 slice-start.1
  283.6 1.3 multiply_convert_fusion
  285.0 0.0 slice-done
  285.0 0.9 slice-done.1
  285.8 11.0 %fusion.5 = f32[1024,2048]{1,0:T(8,128)} fusion(bf16[2048,1024]{0,1:T(8,128)(2,1)S(1)} %bitcast.40, bf16[2048,2048]{1,0:T(8,128)(2,1)S(1)} %bitcast.42), kind=kOutput, calls=%fused_computation.13 | convolution fusion | flops 8589934592 | bytes 20971520 | tf_op jit(solution)/shard_map/dot_general | solution.py:49
  296.9 0.0 reduce-scatter.3.cloned.1.call-done
  296.9 2.3 copy.28
  299.1 72.0 %reduce-scatter.5.cloned.1.call-done = bf16[256,2048]{1,0:T(8,128)(2,1)} async-done(((bf16[256,8192]{1,0:T(8,128)(2,1)}), bf16[256,2048]{1,0:T(8,128)(2,1)}) %reduce-scatter.5.cloned.1.call-update) | async-done | bytes 1048592 | tf_op jit(solution)/shard_map/reduce_scatter | solution.py:39
  (1 shorter events, 0.0 us)
Async XLA Ops:
  7.2 86.5 %all-gather.3.cloned.1.call-start = ((), (), s32[]{:S(2)}) async-start(), calls=%async_computation.4 | async-start | bytes 5242880 | tf_op jit(solution)/shard_map/all_gather | solution.py:26
  9.5 176.0 %all-gather.5.cloned.1.call-start = ((), (), s32[]{:S(2)}) async-start(), calls=%async_computation.6 | async-start | bytes 9437184 | tf_op jit(solution)/shard_map/all_gather | solution.py:25
  93.6 71.2 %all-to-all-start = ((bf16[256,8,1024]{0,2,1:T(8,128)(2,1)}), bf16[256,8,1024]{0,2,1:T(8,128)(2,1)}, u32[]{:S(2)}, u32[]{:S(2)}) async-start(bf16[256,8,1024]{0,2,1:T(8,128)(2,1)} %bitcast.35), calls=%async_computation | async-start | bytes 8388608 | tf_op jit(solution)/shard_map/all_to_all | solution.py:27
  98.2 198.6 %reduce-scatter.3.cloned.1.call-start = ((), (), s32[]{:S(2)}) async-start(), calls=%async_computation.5 | async-start | bytes 9437184 | tf_op jit(solution)/shard_map/reduce_scatter | solution.py:42
  185.4 185.6 %reduce-scatter.5.cloned.1.call-start = ((), (), s32[]{:S(2)}) async-start(), calls=%async_computation.7 | async-start | bytes 5242880 | tf_op jit(solution)/shard_map/reduce_scatter | solution.py:39
  280.1 4.8 %slice-start = ((s8[8388608]{0:T(1024)(128)(4,1)}), s8[4194304]{0:T(1024)(128)(4,1)S(1)}, s32[]{:S(2)}) async-start(s8[8388608]{0:T(1024)(128)(4,1)} %bitcast.41), calls=%async_computation.8 | async-start | bytes 8388608
  283.6 2.2 slice-start.1
Sparse Core Ops, SparseCore 0:
  10.1 83.4 all-gather.2
  95.5 87.3 all-gather.4
  186.4 105.0 reduce-scatter.2
  294.3 76.7 reduce-scatter.4

commit v2 on v1

--- a/solution.py
+++ b/solution.py
@@ -1,6 +1,10 @@
+import functools
+
 import jax
 import jax.numpy as jnp
 from jax import lax
+from jax.experimental import pallas as pl
+from jax.experimental.pallas import tpu as pltpu
 from jax.sharding import PartitionSpec as P
 
 HBLK = 128
@@ -52,8 +56,436 @@
     return outputs, input_grad, grad_rot
 
 
+SUB = 4
+TILE = 512
+GRAD_TILE = 256
+MESH = pl.DeviceIdType.MESH
+
+
+def kernel(n, acts_ref, wrot_ref, up_ref, left_ref, right_ref,
+           out_ref, ig_ref, grad_ref,
+           w_raw, w, x, xo, rot, u, pi, below, above, po, rs_long, rs_short, gt,
+           load_sem, d1_send, d1_recv, x_send, x_recv, xo_send, xo_recv,
+           e_long, e_short, e_sib, u_recv, w_sem, c_send, c_recv, f_send, f_recv,
+           rl_send, rl_recv, rr_send, rr_recv, g_sem):
+    half = n // 2
+    tok, feats = acts_ref.shape
+    rows, cols = wrot_ref.shape
+    sub_tok = tok // SUB
+    pieces = n * SUB
+    l = lax.axis_index("local")
+    z = lax.axis_index("node")
+    p, c = lax.div(l, 2), lax.rem(l, 2)
+    s = 1 - 2 * c
+    column, line = lax.rem(p, 2), lax.div(p, 2)
+    r = column * (n - 1 - line) + (1 - column) * line
+
+    def ring(offset):
+        at = lax.rem(r + offset + 2 * n, n)
+        far = lax.div(at, half)
+        return (1 - far) * (2 * at) + far * (2 * (n - 1 - at) + 1)
+
+    ge = lax.div(z - p + n, n)
+    le = lax.div(p - z + n, n)
+    home = ge * le
+    dist = (1 - le) * (z - p) + (1 - ge) * (p - z)
+    upper = lax.div(2 * p, n)
+    c_lag = (1 - ge) * z + (1 - le) * (n - 1 - z) + home * (
+        upper * p + (1 - upper) * (n - 1 - p))
+    goes_up = jnp.logical_and(z >= p, z < n - 1)
+    goes_down = jnp.logical_and(z <= p, z > 0)
+    from_below = goes_down
+    from_above = goes_up
+
+    def dev(chip, core, node):
+        return {"local": 2 * chip + core, "node": node}
+
+    sibling = dev(p, 1 - c, z)
+    long_nb, short_nb = dev(ring(s), c, z), dev(ring(-s), c, z)
+
+    def remote(src, dst, send, recv, to):
+        return pltpu.make_async_remote_copy(
+            src_ref=src, dst_ref=dst, send_sem=send, recv_sem=recv,
+            device_id=to, device_id_type=MESH)
+
+    def u_rows(index):
+        return pl.ds(pl.multiple_of(index * tok, tok), tok)
+
+    def part(index):
+        return pl.ds(pl.multiple_of(index * sub_tok, sub_tok), sub_tok)
+
+    barrier = pltpu.get_barrier_semaphore()
+    for k in range(1, n):
+        pl.semaphore_signal(barrier, inc=1, device_id=dev(ring(k), c, z), device_id_type=MESH)
+    pl.semaphore_signal(barrier, inc=1, device_id=sibling, device_id_type=MESH)
+
+    @pl.when(z > 0)
+    def _():
+        pl.semaphore_signal(barrier, inc=1, device_id=dev(p, c, z - 1), device_id_type=MESH)
+
+    @pl.when(z < n - 1)
+    def _():
+        pl.semaphore_signal(barrier, inc=1, device_id=dev(p, c, z + 1), device_id_type=MESH)
+
+    load_w = pltpu.make_async_copy(wrot_ref, w_raw, load_sem.at[0])
+    load_w.start()
+    load_u = pltpu.make_async_copy(up_ref, u.at[u_rows(l)], load_sem.at[1])
+    load_u.start()
+    load_x = pltpu.make_async_copy(acts_ref, x.at[p], load_sem.at[2])
+
+    @pl.when(home == 1)
+    def _():
+        load_x.start()
+
+    pl.semaphore_wait(barrier, n + 2 - lax.div(n - z, n) - lax.div(z + 1, n))
+
+    d1 = remote(acts_ref, x.at[p], d1_send, d1_recv.at[p], dev(z, c, z))
+
+    @pl.when(home == 0)
+    def _():
+        d1.start()
+
+    load_u.wait()
+
+    def e_copy_long(step):
+        at = u_rows(2 * ring(-s * (step - 1)) + c)
+        return remote(u.at[at], u.at[at], e_long.at[step - 1],
+                      u_recv.at[2 * ring(-s * (step - 1)) + c], long_nb)
+
+    def e_copy_short(step):
+        at = u_rows(2 * ring(s * (step - 1)) + c)
+        return remote(u.at[at], u.at[at], e_short.at[step - 1],
+                      u_recv.at[2 * ring(s * (step - 1)) + c], short_nb)
+
+    def e_copy_sib(chip):
+        at = u_rows(2 * chip + c)
+        return remote(u.at[at], u.at[at], e_sib.at[chip], u_recv.at[2 * chip + c], sibling)
+
+    def u_arrived(index):
+        pltpu.make_async_copy(u.at[u_rows(index)], u.at[u_rows(index)], u_recv.at[index]).wait()
+
+    e_copy_long(1).start()
+    e_copy_short(1).start()
+
+    load_w.wait()
+    own_rows = pl.ds(pl.multiple_of(c * rows, rows), rows)
+
+    @pl.loop(0, rows // HBLK)
+    def _(b):
+        at = pl.ds(pl.multiple_of(b * HBLK, HBLK), HBLK)
+        to = pl.ds(pl.multiple_of(c * rows + b * HBLK, HBLK), HBLK)
+        mixed = jnp.dot(left_ref[b], w_raw[at, :], preferred_element_type=jnp.float32)
+        w[to, :] = (mixed * (1.0 / HBLK)).astype(jnp.bfloat16)
+
+    w_copy = remote(w.at[own_rows], w.at[own_rows], w_sem.at[0], w_sem.at[1], sibling)
+    w_copy.start()
+    e_copy_sib(p).start()
+
+    def x_chip(i):
+        moved = lax.div(i + n - 1, n) * (half - lax.div(i, 2)) * (1 - 2 * lax.rem(i, 2))
+        return ring(moved * s)
+
+    def c_chip(i):
+        return ring(lax.div(i + 1, 2) * (1 - 2 * lax.rem(i, 2)) * s)
+
+    def x_copy(q, sub, way, node):
+        at = part(sub)
+        return remote(x.at[q, at], x.at[q, at], x_send.at[way, q * SUB + sub],
+                      x_recv.at[q * SUB + sub], dev(p, c, node))
+
+    def xo_copy(q):
+        cut = pl.ds(pl.multiple_of((1 - c) * rows, rows), rows)
+        return remote(x.at[q, :, cut], xo.at[q], xo_send.at[q], xo_recv.at[q], sibling)
+
+    def c_copy_up(q, sub):
+        return remote(pi.at[q, part(sub)], below.at[q, part(sub)], c_send.at[q * SUB + sub],
+                      c_recv.at[0, q * SUB + sub], dev(p, c, z + 1))
+
+    def c_copy_down(q, sub):
+        return remote(pi.at[q, part(sub)], above.at[q, part(sub)], c_send.at[q * SUB + sub],
+                      c_recv.at[1, q * SUB + sub], dev(p, c, z - 1))
+
+    def f_copy(q, sub):
+        return remote(pi.at[q, part(sub)], ig_ref.at[part(sub)], f_send.at[q * SUB + sub],
+                      f_recv.at[sub], dev(q, c, z))
+
+    def rl_copy(k):
+        return remote(po.at[ring(s * k)], rs_long.at[k - 1], rl_send.at[k - 1],
+                      rl_recv.at[k - 1], long_nb)
+
+    def rr_copy(k):
+        return remote(po.at[ring(-s * k)], rs_short.at[k - 1], rr_send.at[k - 1],
+                      rr_recv.at[k - 1], short_nb)
+
+    def rotate(q, index, read):
+        at = pl.ds(pl.multiple_of(index * tok, tok), tok)
+        for b in range(rows // HBLK):
+            turned = lax.dot_general(right_ref[b], read(b), (((1,), (1,)), ((), ())),
+                                     preferred_element_type=jnp.float32)
+            rot[b * HBLK:(b + 1) * HBLK, at] = (turned * (1.0 / HBLK)).astype(jnp.bfloat16)
+
+    def add_into(total, piece):
+        return (total.astype(jnp.float32) + piece.astype(jnp.float32)).astype(jnp.bfloat16)
+
+    c_start = 2
+    slots = c_start + n - 1 + pieces
+
+    @pl.loop(0, slots)
+    def _(t):
+        @pl.when(t == c_start)
+        def _():
+            w_copy.wait_recv()
+
+        for step in range(1, half + 1):
+            @pl.when(t == SUB * step)
+            def _(step=step):
+                first = ring(-s * step)
+                u_arrived(2 * first + c)
+                if step < half:
+                    e_copy_long(step + 1).start()
+                e_copy_sib(first).start()
+                if step < half:
+                    second = ring(s * step)
+                    u_arrived(2 * second + c)
+                    if step < half - 1:
+                        e_copy_short(step + 1).start()
+                    e_copy_sib(second).start()
+
+        j = t - dist
+
+        @pl.when(jnp.logical_and(j >= 0, j < pieces))
+        def _():
+            i, sub = lax.div(j, SUB), lax.rem(j, SUB)
+            q = x_chip(i)
+
+            @pl.when(jnp.logical_and(home == 1, j == 0))
+            def _():
+                load_x.wait()
+
+            @pl.when(jnp.logical_and(home == 1, jnp.logical_and(sub == 0, j > 0)))
+            def _():
+                pltpu.make_async_copy(x.at[q], x.at[q], d1_recv.at[q]).wait()
+
+            @pl.when(home == 0)
+            def _():
+                pltpu.make_async_copy(x.at[q, part(sub)], x.at[q, part(sub)],
+                                      x_recv.at[q * SUB + sub]).wait()
+
+            @pl.when(goes_up)
+            def _():
+                x_copy(q, sub, 0, z + 1).start()
+
+            @pl.when(goes_down)
+            def _():
+                x_copy(q, sub, 1, z - 1).start()
+
+            @pl.when(sub == SUB - 1)
+            def _():
+                xo_copy(q).start()
+
+                @pl.loop(0, cols // TILE)
+                def _(tile):
+                    at = pl.ds(pl.multiple_of(tile * TILE, TILE), TILE)
+                    po[q, :, at] = jnp.dot(
+                        x[q], w[:, at], preferred_element_type=jnp.float32).astype(jnp.bfloat16)
+
+                rotate(q, 2 * q + c, lambda b: x[
+                    q, :, pl.ds(pl.multiple_of(c * rows + b * HBLK, HBLK), HBLK)])
+
+        jc = t - c_start - c_lag
+
+        @pl.when(jnp.logical_and(jc >= 0, jc < pieces))
+        def _():
+            i, sub = lax.div(jc, SUB), lax.rem(jc, SUB)
+            q = c_chip(i)
+            at = part(sub)
+
+            @pl.when(sub == 0)
+            def _():
+                @pl.loop(0, feats // TILE)
+                def _(tile):
+                    cut = pl.ds(pl.multiple_of(tile * TILE, TILE), TILE)
+                    pi[q, :, cut] = lax.dot_general(
+                        u[u_rows(2 * q + c), :], w[cut, :], (((1,), (1,)), ((), ())),
+                        preferred_element_type=jnp.float32).astype(jnp.bfloat16)
+
+            @pl.when(from_below)
+            def _():
+                pltpu.make_async_copy(below.at[q, at], below.at[q, at],
+                                      c_recv.at[0, q * SUB + sub]).wait()
+                pi[q, at, :] = add_into(pi[q, at, :], below[q, at, :])
+
+            @pl.when(from_above)
+            def _():
+                pltpu.make_async_copy(above.at[q, at], above.at[q, at],
+                                      c_recv.at[1, q * SUB + sub]).wait()
+                pi[q, at, :] = add_into(pi[q, at, :], above[q, at, :])
+
+            @pl.when(z < p)
+            def _():
+                c_copy_up(q, sub).start()
+
+            @pl.when(z > p)
+            def _():
+                c_copy_down(q, sub).start()
+
+            @pl.when(jnp.logical_and(home == 1, q == p))
+            def _():
+                ig_ref[at, :] = pi[q, at, :]
+
+            @pl.when(jnp.logical_and(home == 1, q != p))
+            def _():
+                f_copy(q, sub).start()
+
+        for k in range(half, 0, -1):
+            i = 1 if k == half else 2 * (half - k)
+
+            @pl.when(t == n - 1 + SUB * i + SUB - 1)
+            def _(k=k):
+                if k < half:
+                    rl_copy(k + 1).wait_recv()
+                    q = ring(s * k)
+                    po[q] = add_into(po[q], rs_long[k])
+                rl_copy(k).start()
+
+        for k in range(half - 1, 0, -1):
+            @pl.when(t == n - 1 + SUB * (2 * (half - k) + 1) + SUB - 1)
+            def _(k=k):
+                if k < half - 1:
+                    rr_copy(k + 1).wait_recv()
+                    q = ring(-s * k)
+                    po[q] = add_into(po[q], rs_short[k])
+                rr_copy(k).start()
+
+    @pl.loop(0, n)
+    def _(q):
+        pltpu.make_async_copy(xo.at[q], xo.at[q], xo_recv.at[q]).wait()
+        u_arrived(2 * q + 1 - c)
+        rotate(q, 2 * q + 1 - c, lambda b: xo[q, :, b * HBLK:(b + 1) * HBLK])
+
+    def g_copy(tile, slot):
+        at = pl.ds(pl.multiple_of(tile * GRAD_TILE, GRAD_TILE), GRAD_TILE)
+        return pltpu.make_async_copy(gt.at[slot], grad_ref.at[:, at], g_sem.at[slot])
+
+    tiles = cols // GRAD_TILE
+
+    @pl.loop(0, tiles)
+    def _(tile):
+        slot = lax.rem(tile, 2)
+
+        @pl.when(tile >= 2)
+        def _():
+            g_copy(tile - 2, slot).wait()
+
+        at = pl.ds(pl.multiple_of(tile * GRAD_TILE, GRAD_TILE), GRAD_TILE)
+        gt[slot] = jnp.dot(rot[...], u[:, at], preferred_element_type=jnp.float32)
+        g_copy(tile, slot).start()
+
+    rl_copy(1).wait_recv()
+    rr_copy(1).wait_recv()
+    out_ref[...] = (po[p].astype(jnp.float32) + rs_long[0].astype(jnp.float32)
+                    + rs_short[0].astype(jnp.float32)).astype(jnp.bfloat16)
+
+    @pl.when(home == 0)
+    def _():
+        for sub in range(SUB):
+            pltpu.make_async_copy(ig_ref.at[part(sub)], ig_ref.at[part(sub)], f_recv.at[sub]).wait()
+        d1.wait_send()
+
+    for tile in (tiles - 2, tiles - 1):
+        g_copy(tile, tile % 2).wait()
+    w_copy.wait_send()
+    for step in range(1, half + 1):
+        e_copy_long(step).wait_send()
+        rl_copy(step).wait_send()
+    for step in range(1, half):
+        e_copy_short(step).wait_send()
+        rr_copy(step).wait_send()
+
+    @pl.loop(0, n)
+    def _(q):
+        e_copy_sib(q).wait_send()
+        xo_copy(q).wait_send()
+
+        @pl.loop(0, SUB)
+        def _(sub):
+            @pl.when(goes_up)
+            def _():
+                x_copy(q, sub, 0, z + 1).wait_send()
+
+            @pl.when(goes_down)
+            def _():
+                x_copy(q, sub, 1, z - 1).wait_send()
+
+            @pl.when(z < p)
+            def _():
+                c_copy_up(q, sub).wait_send()
+
+            @pl.when(z > p)
+            def _():
+                c_copy_down(q, sub).wait_send()
+
+            @pl.when(jnp.logical_and(home == 1, q != p))
+            def _():
+                f_copy(q, sub).wait_send()
+
+
+def fused(acts, w_rot, signs, upstream):
+    n = lax.axis_size("node")
+    tok, feats = acts.shape
+    rows, cols = w_rot.shape
+    blocks = rows // HBLK
+    half = n // 2
+    had = sylvester(HBLK)
+    own_signs = lax.dynamic_slice_in_dim(signs, lax.axis_index("local") * rows, rows)
+    own_signs = own_signs.astype(jnp.float32).reshape(blocks, HBLK)
+    left = (own_signs[:, :, None] * had).astype(jnp.bfloat16)
+    right = (own_signs[:, None, :] * had).astype(jnp.bfloat16)
+    bf = jnp.bfloat16
+    dma = pltpu.SemaphoreType.DMA
+    vmem = pl.BlockSpec(memory_space=pltpu.VMEM)
+    hbm = pl.BlockSpec(memory_space=pl.ANY)
+    tokens = 2 * n * tok
+    return pl.pallas_call(
+        functools.partial(kernel, n),
+        out_shape=(
+            jax.ShapeDtypeStruct((tok, cols), bf),
+            jax.ShapeDtypeStruct((tok, feats), bf),
+            jax.ShapeDtypeStruct((rows, cols), jnp.float32),
+        ),
+        in_specs=[hbm, hbm, hbm, vmem, vmem],
+        out_specs=(vmem, vmem, hbm),
+        scratch_shapes=[
+            pltpu.VMEM((rows, cols), bf),
+            pltpu.VMEM((feats, cols), bf),
+            pltpu.VMEM((n, tok, feats), bf),
+            pltpu.VMEM((n, tok, rows), bf),
+            pltpu.VMEM((rows, tokens), bf),
+            pltpu.VMEM((tokens, cols), bf),
+            pltpu.VMEM((n, tok, feats), bf),
+            pltpu.VMEM((n, tok, feats), bf),
+            pltpu.VMEM((n, tok, feats), bf),
+            pltpu.VMEM((n, tok, cols), bf),
+            pltpu.VMEM((half, tok, cols), bf),
+            pltpu.VMEM((half - 1, tok, cols), bf),
+            pltpu.VMEM((2, rows, GRAD_TILE), jnp.float32),
+            dma((3,)), dma, dma((n,)), dma((2, n * SUB)), dma((n * SUB,)), dma((n,)), dma((n,)),
+            dma((half,)), dma((half - 1,)), dma((n,)), dma((2 * n,)), dma((2,)),
+            dma((n * SUB,)), dma((2, n * SUB)), dma((n * SUB,)), dma((SUB,)),
+            dma((half,)), dma((half,)), dma((half - 1,)), dma((half - 1,)), dma((2,)),
+        ],
+        compiler_params=pltpu.CompilerParams(
+            collective_id=0, has_side_effects=True, vmem_limit_bytes=60 << 20),
+        cost_estimate=pl.CostEstimate(
+            flops=6 * tokens * rows * cols, bytes_accessed=16 * rows * cols, transcendentals=0),
+    )(acts, w_rot, upstream, left, right)
+
+
 def solution(mesh):
     spec = P("local", "node")
+    n = mesh.shape["node"]
+    paired = mesh.shape["local"] == 2 * n and n >= 4 and n % 2 == 0
     return jax.shard_map(
-        local, mesh=mesh, in_specs=(spec, spec, P(), spec), out_specs=(spec, spec, spec), check_vma=False
+        fused if paired else local, mesh=mesh, in_specs=(spec, spec, P(), spec),
+        out_specs=(spec, spec, spec), check_vma=False,
     )

time: 378 us -> 215 us (0.57)
  waiting for transfers between devices: 216 us -> 0 us
  Pallas kernels: 0 us -> 200 us
  blocking collectives: 74.8 us -> 0 us
  matrix products: 45.3 us -> 0 us
  between operations: 13.8 us -> 0.65 us
  local copies, waits for them, and re-layouts: 22.1 us -> 12.5 us
  starting transfers between devices: 4.74 us -> 0 us
    pallas_call x0 -> x1, Pallas kernels: none -> 200 us  [fused(): pl.pallas_call(functools.partial(kernel, n), out_shape=(jax.ShapeDtypeStr...]
    all_gather x2 -> x0, waiting for transfers between devices: 83.4 us -> none  [the longest x1 83.4 us: local(): feats = lax.all_gather(acts, 'node', axis=1, tiled=True)]
    all_to_all x1 -> x0, blocking collectives: 74.8 us -> none  [local(): lax.all_to_all(terms, 'local', split_axis=0, concat_axis=1, tiled=True)]
    reduce_scatter x2 -> x0, waiting for transfers between devices: 72 us -> none  [the longest x1 72 us: local(): lax.psum_scatter(terms, 'node', scatter_dimension=1, tiled=True)]
    all_to_all x1 -> x0, waiting for transfers between devices: 60 us -> none  [local(): lax.all_to_all(feats, 'local', split_axis=1, concat_axis=0, tiled=True)]
    dot_general x5 -> x0, matrix products: 45.3 us -> none  [the longest x1 14.1 us: local(): jnp.dot(own, weight, preferred_element_type=jnp.float32)]
    all_to_all x3 -> x0, local copies, waits for them, and re-layouts: 13.2 us -> none  [the longest x2 6.74 us: local(): lax.all_to_all(terms, 'local', split_axis=0, concat_axis=1, tiled=True)]
    all_to_all x1 -> x0, starting transfers between devices: 4.58 us -> none  [local(): lax.all_to_all(feats, 'local', split_axis=1, concat_axis=0, tiled=True)]
  transfers between devices with their start and end apart: 5 -> 0, of which waited for: 3 -> 0; matrix products, arithmetic and copies ran while one was open for 17% -> 0% of each run, Pallas kernels for 0% -> 0%
where the time goes in v2:
time: 215 us; the launch traced here: 214 us
  Pallas kernels  200 us (93%)
  local copies, waits for them, and re-layouts  12.5 us (6%)
    pallas_call x1, Pallas kernels, fused(): pl.pallas_call(functools.partial(kernel, n), out_shape=(jax.ShapeDtypeStr...  200 us
    unnamed x3, local copies, waits for them, and re-layouts  12.5 us

profile of v2, /device:TPU:0, one launch (start us, length us, event | category | flops | bytes accessed | tf_op | source)
XLA Modules:
  0.0 214.5 jit_solution(4459555036869486478)
XLA Ops:
  0.6 0.7 convert_bitcast_fusion
  1.3 0.1 subtract_convert_fusion
  1.4 1.0 multiply_convert_fusion
  2.4 199.6 %shard_map.67 = (bf16[256,2048]{1,0:T(8,128)(2,1)}, bf16[256,2048]{1,0:T(8,128)(2,1)}, f32[1024,2048]{1,0:T(8,128)}) custom-call(bf16[256,2048]{1,0:T(8,128)(2,1)} %acts_ref.1, bf16[1024,2048]{1,0:T(8,128)(2,1)} %wrot_ref.1, bf16[256,2048]{1,0:T(8,128)(2,1)} %up_ref.1, bf16[8,128,128]{2,1,0:T(8,128)(2,1)} %get-tuple-element.4.left_ref, ...), custom_call_target="tpu_custom_call" | custom-call | flops 25769803776 | bytes 33554432 | tf_op jit(solution)/shard_map/pallas_call | solution.py:449
  202.0 2.3 %copy.10 = bf16[256,2048]{1,0:T(8,128)(2,1)} copy(bf16[256,2048]{1,0:T(8,128)(2,1)} %get-tuple-element.8) | data formatting | bytes 2097152
  204.3 2.3 %copy.11 = bf16[256,2048]{1,0:T(8,128)(2,1)} copy(bf16[256,2048]{1,0:T(8,128)(2,1)} %get-tuple-element.9) | data formatting | bytes 2097152
  206.6 7.9 %copy.12 = f32[1024,2048]{1,0:T(8,128)} copy(f32[1024,2048]{1,0:T(8,128)} %get-tuple-element.10) | data formatting | bytes 16777216

commit v3 on v2

--- a/solution.py
+++ b/solution.py
@@ -141,7 +141,14 @@
 
     d1 = remote(acts_ref, x.at[p], d1_send, d1_recv.at[p], dev(z, c, z))
 
-    @pl.when(home == 0)
+    home_column, home_line = lax.rem(z, 2), lax.div(z, 2)
+    home_r = home_column * (n - 1 - home_line) + (1 - home_column) * home_line
+    away = lax.rem(s * (r - home_r) + 2 * n, n)
+    past = lax.div(away + half - 1, n)
+    arc = past * (n - away) + (1 - past) * away
+    turn = 2 * (half - arc) + past + lax.div(arc, half)
+
+    @pl.when(jnp.logical_and(home == 0, turn == 1))
     def _():
         d1.start()
 
@@ -165,21 +172,8 @@
         pltpu.make_async_copy(u.at[u_rows(index)], u.at[u_rows(index)], u_recv.at[index]).wait()
 
     e_copy_long(1).start()
-    e_copy_short(1).start()
-
-    load_w.wait()
     own_rows = pl.ds(pl.multiple_of(c * rows, rows), rows)
-
-    @pl.loop(0, rows // HBLK)
-    def _(b):
-        at = pl.ds(pl.multiple_of(b * HBLK, HBLK), HBLK)
-        to = pl.ds(pl.multiple_of(c * rows + b * HBLK, HBLK), HBLK)
-        mixed = jnp.dot(left_ref[b], w_raw[at, :], preferred_element_type=jnp.float32)
-        w[to, :] = (mixed * (1.0 / HBLK)).astype(jnp.bfloat16)
-
     w_copy = remote(w.at[own_rows], w.at[own_rows], w_sem.at[0], w_sem.at[1], sibling)
-    w_copy.start()
-    e_copy_sib(p).start()
 
     def x_chip(i):
         moved = lax.div(i + n - 1, n) * (half - lax.div(i, 2)) * (1 - 2 * lax.rem(i, 2))
@@ -224,10 +218,20 @@
                                      preferred_element_type=jnp.float32)
             rot[b * HBLK:(b + 1) * HBLK, at] = (turned * (1.0 / HBLK)).astype(jnp.bfloat16)
 
+    def rotate_own(q):
+        rotate(q, 2 * q + c, lambda b: x[
+            q, :, pl.ds(pl.multiple_of(c * rows + b * HBLK, HBLK), HBLK)])
+
+    def out_tile(q, tile):
+        at = pl.ds(pl.multiple_of(tile * tile_cols, tile_cols), tile_cols)
+        po[q, :, at] = jnp.dot(
+            x[q], w[:, at], preferred_element_type=jnp.float32).astype(jnp.bfloat16)
+
     def add_into(total, piece):
         return (total.astype(jnp.float32) + piece.astype(jnp.float32)).astype(jnp.bfloat16)
 
-    c_start = 2
+    c_start = 3
+    tile_cols = cols // SUB
     slots = c_start + n - 1 + pieces
 
     @pl.loop(0, slots)
@@ -236,20 +240,31 @@
         def _():
             w_copy.wait_recv()
 
+        @pl.when(jnp.logical_and(t == SUB * turn - 5, jnp.logical_and(home == 0, turn > 1)))
+        def _():
+            d1.start()
+
+        @pl.when(t == 2)
+        def _():
+            e_copy_short(1).start()
+
         for step in range(1, half + 1):
-            @pl.when(t == SUB * step)
+            @pl.when(t == SUB * (2 * step - 1) + 1)
             def _(step=step):
-                first = ring(-s * step)
-                u_arrived(2 * first + c)
+                source = ring(-s * step)
+                u_arrived(2 * source + c)
                 if step < half:
                     e_copy_long(step + 1).start()
-                e_copy_sib(first).start()
-                if step < half:
-                    second = ring(s * step)
-                    u_arrived(2 * second + c)
-                    if step < half - 1:
-                        e_copy_short(step + 1).start()
-                    e_copy_sib(second).start()
+                e_copy_sib(source).start()
+
+        for step in range(1, half):
+            @pl.when(t == 2 * SUB * step + 1)
+            def _(step=step):
+                source = ring(s * step)
+                u_arrived(2 * source + c)
+                if step < half - 1:
+                    e_copy_short(step + 1).start()
+                e_copy_sib(source).start()
 
         j = t - dist
 
@@ -283,14 +298,35 @@
             def _():
                 xo_copy(q).start()
 
-                @pl.loop(0, cols // TILE)
+            @pl.when(jnp.logical_and(i > 0, sub < 2))
+            def _():
+                done = x_chip(i - 1)
+                for tile in range(SUB // 2):
+                    out_tile(done, sub * (SUB // 2) + tile)
+
+            @pl.when(jnp.logical_and(i > 0, sub == 2))
+            def _():
+                rotate_own(x_chip(i - 1))
+
+            @pl.when(j == pieces - 1)
+            def _():
+                @pl.loop(0, SUB)
                 def _(tile):
-                    at = pl.ds(pl.multiple_of(tile * TILE, TILE), TILE)
-                    po[q, :, at] = jnp.dot(
-                        x[q], w[:, at], preferred_element_type=jnp.float32).astype(jnp.bfloat16)
-
-                rotate(q, 2 * q + c, lambda b: x[
-                    q, :, pl.ds(pl.multiple_of(c * rows + b * HBLK, HBLK), HBLK)])
+                    out_tile(q, tile)
+
+        @pl.when(t == 0)
+        def _():
+            load_w.wait()
+
+            @pl.loop(0, rows // HBLK)
+            def _(b):
+                at = pl.ds(pl.multiple_of(b * HBLK, HBLK), HBLK)
+                to = pl.ds(pl.multiple_of(c * rows + b * HBLK, HBLK), HBLK)
+                mixed = jnp.dot(left_ref[b], w_raw[at, :], preferred_element_type=jnp.float32)
+                w[to, :] = (mixed * (1.0 / HBLK)).astype(jnp.bfloat16)
+
+            w_copy.start()
+            e_copy_sib(p).start()
 
         jc = t - c_start - c_lag
 
@@ -340,7 +376,7 @@
         for k in range(half, 0, -1):
             i = 1 if k == half else 2 * (half - k)
 
-            @pl.when(t == n - 1 + SUB * i + SUB - 1)
+            @pl.when(t == n - 1 + SUB * i + SUB + 1)
             def _(k=k):
                 if k < half:
                     rl_copy(k + 1).wait_recv()
@@ -349,13 +385,15 @@
                 rl_copy(k).start()
 
         for k in range(half - 1, 0, -1):
-            @pl.when(t == n - 1 + SUB * (2 * (half - k) + 1) + SUB - 1)
+            @pl.when(t == n - 1 + SUB * (2 * (half - k) + 1) + SUB - 1 + 2 * min(k - 1, 1))
             def _(k=k):
                 if k < half - 1:
                     rr_copy(k + 1).wait_recv()
                     q = ring(-s * k)
                     po[q] = add_into(po[q], rs_short[k])
                 rr_copy(k).start()
+
+    rotate_own(x_chip(n - 1))
 
     @pl.loop(0, n)
     def _(q):
@@ -428,6 +466,33 @@
             @pl.when(jnp.logical_and(home == 1, q != p))
             def _():
                 f_copy(q, sub).wait_send()
+
+
+COPY_PARTS = 8
+
+
+def copy_kernel(out_ref, ig_ref, grad_ref, out_to, ig_to, grad_to, sems):
+    copies = [pltpu.make_async_copy(out_ref, out_to, sems.at[0]),
+              pltpu.make_async_copy(ig_ref, ig_to, sems.at[1])]
+    rows = grad_ref.shape[0] // COPY_PARTS
+    for part in range(COPY_PARTS):
+        at = pl.ds(part * rows, rows)
+        copies.append(pltpu.make_async_copy(grad_ref.at[at], grad_to.at[at], sems.at[2 + part]))
+    for copy in copies:
+        copy.start()
+    for copy in copies:
+        copy.wait()
+
+
+def hand_on(arrays):
+    hbm = pl.BlockSpec(memory_space=pl.ANY)
+    return pl.pallas_call(
+        copy_kernel,
+        out_shape=tuple(jax.ShapeDtypeStruct(a.shape, a.dtype) for a in arrays),
+        in_specs=[hbm] * 3,
+        out_specs=(hbm,) * 3,
+        scratch_shapes=[pltpu.SemaphoreType.DMA((2 + COPY_PARTS,))],
+    )(*arrays)
 
 
 def fused(acts, w_rot, signs, upstream):
@@ -446,7 +511,7 @@
     vmem = pl.BlockSpec(memory_space=pltpu.VMEM)
     hbm = pl.BlockSpec(memory_space=pl.ANY)
     tokens = 2 * n * tok
-    return pl.pallas_call(
+    return hand_on(pl.pallas_call(
         functools.partial(kernel, n),
         out_shape=(
             jax.ShapeDtypeStruct((tok, cols), bf),
@@ -478,7 +543,7 @@
             collective_id=0, has_side_effects=True, vmem_limit_bytes=60 << 20),
         cost_estimate=pl.CostEstimate(
             flops=6 * tokens * rows * cols, bytes_accessed=16 * rows * cols, transcendentals=0),
-    )(acts, w_rot, upstream, left, right)
+    )(acts, w_rot, upstream, left, right))
 
 
 def solution(mesh):

time: 215 us -> 500 us (2.33)
  Pallas kernels: 200 us -> 495 us
  local copies, waits for them, and re-layouts: 12.5 us -> 0 us
    pallas_call x0 -> x1, Pallas kernels: none -> 319 us  [hand_on(): pl.pallas_call(copy_kernel, out_shape=tuple((jax.ShapeDtypeStruct(a.shape...]
    pallas_call x1, Pallas kernels: 200 us -> 176 us  [fused(): pl.pallas_call(functools.partial(kernel, n), out_shape=(jax.ShapeDtypeStr...]
    unnamed x3 -> x0, local copies, waits for them, and re-layouts: 12.5 us -> none
where the time goes in v3:
time: 500 us; the launch traced here: 497 us
  Pallas kernels  495 us (99%)
    pallas_call x1, Pallas kernels, hand_on(): pl.pallas_call(copy_kernel, out_shape=tuple((jax.ShapeDtypeStruct(a.shape...  319 us
    pallas_call x1, Pallas kernels, fused(): pl.pallas_call(functools.partial(kernel, n), out_shape=(jax.ShapeDtypeStr...  176 us

profile of v3, /device:TPU:0, one launch (start us, length us, event | category | flops | bytes accessed | tf_op | source)
XLA Modules:
  0.0 497.4 jit_solution(237845646283180137)
XLA Ops:
  0.6 0.7 convert_bitcast_fusion
  1.3 0.1 subtract_convert_fusion
  1.4 1.0 multiply_convert_fusion
  2.4 176.2 %shard_map.67 = (bf16[256,2048]{1,0:T(8,128)(2,1)}, bf16[256,2048]{1,0:T(8,128)(2,1)}, f32[1024,2048]{1,0:T(8,128)}) custom-call(bf16[256,2048]{1,0:T(8,128)(2,1)} %acts_ref.1, bf16[1024,2048]{1,0:T(8,128)(2,1)} %wrot_ref.1, bf16[256,2048]{1,0:T(8,128)(2,1)} %up_ref.1, bf16[8,128,128]{2,1,0:T(8,128)(2,1)} %get-tuple-element.10.left_ref, ...), custom_call_target="tpu_custom_call" | custom-call | flops 25769803776 | bytes 33554432 | tf_op jit(solution)/shard_map/pallas_call | solution.py:514
  178.5 318.8 %shard_map.68 = (bf16[256,2048]{1,0:T(8,128)(2,1)}, bf16[256,2048]{1,0:T(8,128)(2,1)}, f32[1024,2048]{1,0:T(8,128)}) custom-call(bf16[256,2048]{1,0:T(8,128)(2,1)} %get-tuple-element.6.out_ref, bf16[256,2048]{1,0:T(8,128)(2,1)} %get-tuple-element.7.ig_ref, f32[1024,2048]{1,0:T(8,128)} %get-tuple-element.8.grad_ref), custom_call_target="tpu_custom_call" | custom-call | tf_op jit(solution)/shard_map/pallas_call | solution.py:489

commit v4 on v3

--- a/solution.py
+++ b/solution.py
@@ -56,10 +56,17 @@
     return outputs, input_grad, grad_rot
 
 
-SUB = 4
+SUB = 8
+TILES = 4
 TILE = 512
 GRAD_TILE = 256
 MESH = pl.DeviceIdType.MESH
+
+
+def swapped(n, i):
+    one = lax.div(i + n - 1, n) - lax.div(i + n - 2, n)
+    two = lax.div(i + n - 2, n) - lax.div(i + n - 3, n)
+    return i + one - two
 
 
 def kernel(n, acts_ref, wrot_ref, up_ref, left_ref, right_ref,
@@ -146,7 +153,7 @@
     away = lax.rem(s * (r - home_r) + 2 * n, n)
     past = lax.div(away + half - 1, n)
     arc = past * (n - away) + (1 - past) * away
-    turn = 2 * (half - arc) + past + lax.div(arc, half)
+    turn = swapped(n, 2 * (half - arc) + past + lax.div(arc, half))
 
     @pl.when(jnp.logical_and(home == 0, turn == 1))
     def _():
@@ -171,11 +178,11 @@
     def u_arrived(index):
         pltpu.make_async_copy(u.at[u_rows(index)], u.at[u_rows(index)], u_recv.at[index]).wait()
 
-    e_copy_long(1).start()
     own_rows = pl.ds(pl.multiple_of(c * rows, rows), rows)
     w_copy = remote(w.at[own_rows], w.at[own_rows], w_sem.at[0], w_sem.at[1], sibling)
 
     def x_chip(i):
+        i = swapped(n, i)
         moved = lax.div(i + n - 1, n) * (half - lax.div(i, 2)) * (1 - 2 * lax.rem(i, 2))
         return ring(moved * s)
 
@@ -230,8 +237,8 @@
     def add_into(total, piece):
         return (total.astype(jnp.float32) + piece.astype(jnp.float32)).astype(jnp.bfloat16)
 
-    c_start = 3
-    tile_cols = cols // SUB
+    c_start = 4
+    tile_cols = cols // TILES
     slots = c_start + n - 1 + pieces
 
     @pl.loop(0, slots)
@@ -240,16 +247,20 @@
         def _():
             w_copy.wait_recv()
 
-        @pl.when(jnp.logical_and(t == SUB * turn - 5, jnp.logical_and(home == 0, turn > 1)))
+        @pl.when(jnp.logical_and(t == SUB * turn - SUB // 2 - 10, jnp.logical_and(home == 0, turn > 1)))
         def _():
             d1.start()
 
-        @pl.when(t == 2)
+        @pl.when(t == 3)
+        def _():
+            e_copy_long(1).start()
+
+        @pl.when(t == 8)
         def _():
             e_copy_short(1).start()
 
         for step in range(1, half + 1):
-            @pl.when(t == SUB * (2 * step - 1) + 1)
+            @pl.when(t == SUB * (2 * step - 1))
             def _(step=step):
                 source = ring(-s * step)
                 u_arrived(2 * source + c)
@@ -258,7 +269,7 @@
                 e_copy_sib(source).start()
 
         for step in range(1, half):
-            @pl.when(t == 2 * SUB * step + 1)
+            @pl.when(t == 2 * SUB * step)
             def _(step=step):
                 source = ring(s * step)
                 u_arrived(2 * source + c)
@@ -270,14 +281,15 @@
 
         @pl.when(jnp.logical_and(j >= 0, j < pieces))
         def _():
-            i, sub = lax.div(j, SUB), lax.rem(j, SUB)
-            q = x_chip(i)
+            turns, sub = lax.div(j + SUB // 2, SUB), lax.rem(j + SUB // 2, SUB)
+            q = x_chip(lax.rem(turns, n))
 
             @pl.when(jnp.logical_and(home == 1, j == 0))
             def _():
                 load_x.wait()
 
-            @pl.when(jnp.logical_and(home == 1, jnp.logical_and(sub == 0, j > 0)))
+            @pl.when(jnp.logical_and(
+                home == 1, jnp.logical_and(sub == 0, turns < n)))
             def _():
                 pltpu.make_async_copy(x.at[q], x.at[q], d1_recv.at[q]).wait()
 
@@ -294,25 +306,19 @@
             def _():
                 x_copy(q, sub, 1, z - 1).start()
 
-            @pl.when(sub == SUB - 1)
+            @pl.when(jnp.logical_or(j == pieces - 1, jnp.logical_and(sub == SUB - 1, turns > 0)))
             def _():
                 xo_copy(q).start()
 
-            @pl.when(jnp.logical_and(i > 0, sub < 2))
-            def _():
-                done = x_chip(i - 1)
-                for tile in range(SUB // 2):
-                    out_tile(done, sub * (SUB // 2) + tile)
-
-            @pl.when(jnp.logical_and(i > 0, sub == 2))
-            def _():
-                rotate_own(x_chip(i - 1))
-
-            @pl.when(j == pieces - 1)
-            def _():
-                @pl.loop(0, SUB)
-                def _(tile):
-                    out_tile(q, tile)
+            @pl.when(jnp.logical_and(turns > 1, sub < 2))
+            def _():
+                done = x_chip(turns - 1)
+                for tile in range(TILES // 2):
+                    out_tile(done, sub * (TILES // 2) + tile)
+
+            @pl.when(jnp.logical_and(turns > 1, sub == 3))
+            def _():
+                rotate_own(x_chip(turns - 1))
 
         @pl.when(t == 0)
         def _():
@@ -373,10 +379,13 @@
             def _():
                 f_copy(q, sub).start()
 
+        def rs_slot(i):
+            return n - 1 + SUB * i + SUB // 2 + 1
+
         for k in range(half, 0, -1):
-            i = 1 if k == half else 2 * (half - k)
-
-            @pl.when(t == n - 1 + SUB * i + SUB + 1)
+            at = rs_slot(2 if k == half else 2 * (half - k)) + (SUB // 2 + 1) * (k == half - 1)
+
+            @pl.when(t == at)
             def _(k=k):
                 if k < half:
                     rl_copy(k + 1).wait_recv()
@@ -385,7 +394,7 @@
                 rl_copy(k).start()
 
         for k in range(half - 1, 0, -1):
-            @pl.when(t == n - 1 + SUB * (2 * (half - k) + 1) + SUB - 1 + 2 * min(k - 1, 1))
+            @pl.when(t == rs_slot(2 * (half - k) + 1))
             def _(k=k):
                 if k < half - 1:
                     rr_copy(k + 1).wait_recv()
@@ -393,7 +402,11 @@
                     po[q] = add_into(po[q], rs_short[k])
                 rr_copy(k).start()
 
-    rotate_own(x_chip(n - 1))
+    @pl.loop(0, TILES)
+    def _(tile):
+        out_tile(p, tile)
+
+    rotate_own(p)
 
     @pl.loop(0, n)
     def _(q):
@@ -471,27 +484,20 @@
 COPY_PARTS = 8
 
 
-def copy_kernel(out_ref, ig_ref, grad_ref, out_to, ig_to, grad_to, sems):
-    copies = [pltpu.make_async_copy(out_ref, out_to, sems.at[0]),
-              pltpu.make_async_copy(ig_ref, ig_to, sems.at[1])]
-    rows = grad_ref.shape[0] // COPY_PARTS
-    for part in range(COPY_PARTS):
-        at = pl.ds(part * rows, rows)
-        copies.append(pltpu.make_async_copy(grad_ref.at[at], grad_to.at[at], sems.at[2 + part]))
-    for copy in copies:
-        copy.start()
-    for copy in copies:
-        copy.wait()
+def copy_kernel(*refs):
+    for source, target in zip(refs[:3], refs[3:]):
+        target[...] = source[...]
 
 
 def hand_on(arrays):
-    hbm = pl.BlockSpec(memory_space=pl.ANY)
+    specs = [pl.BlockSpec((a.shape[0] // COPY_PARTS, a.shape[1]), lambda i: (i, 0)) for a in arrays]
     return pl.pallas_call(
         copy_kernel,
+        grid=(COPY_PARTS,),
         out_shape=tuple(jax.ShapeDtypeStruct(a.shape, a.dtype) for a in arrays),
-        in_specs=[hbm] * 3,
-        out_specs=(hbm,) * 3,
-        scratch_shapes=[pltpu.SemaphoreType.DMA((2 + COPY_PARTS,))],
+        in_specs=specs,
+        out_specs=tuple(specs),
+        compiler_params=pltpu.CompilerParams(vmem_limit_bytes=32 << 20),
     )(*arrays)
 
 

time: 500 us -> 221 us (0.44)
  Pallas kernels: 495 us -> 212 us
  local copies, waits for them, and re-layouts: 0 us -> 5.82 us
    pallas_call x1, Pallas kernels: 319 us -> 4.97 us  [hand_on(): pl.pallas_call(copy_kernel, grid=(COPY_PARTS,), out_shape=tuple((jax.Shap...]
    pallas_call x1, Pallas kernels: 176 us -> 207 us  [fused(): pl.pallas_call(functools.partial(kernel, n), out_shape=(jax.ShapeDtypeStr...]
    unnamed x0 -> x6, local copies, waits for them, and re-layouts: none -> 5.82 us
where the time goes in v4:
time: 221 us; the launch traced here: 220 us
  Pallas kernels  212 us (96%)
  local copies, waits for them, and re-layouts  5.82 us (3%)
    pallas_call x1, Pallas kernels, fused(): pl.pallas_call(functools.partial(kernel, n), out_shape=(jax.ShapeDtypeStr...  207 us
    unnamed x6, local copies, waits for them, and re-layouts  5.82 us
    pallas_call x1, Pallas kernels, hand_on(): pl.pallas_call(copy_kernel, grid=(COPY_PARTS,), out_shape=tuple((jax.Shap...  4.97 us

profile of v4, /device:TPU:0, one launch (start us, length us, event | category | flops | bytes accessed | tf_op | source)
XLA Modules:
  0.0 220.2 jit_solution(1892769980949976040)
XLA Ops:
  0.6 0.7 convert_bitcast_fusion
  1.3 0.1 subtract_convert_fusion
  1.4 1.0 multiply_convert_fusion
  2.4 207.1 %shard_map.67 = (bf16[256,2048]{1,0:T(8,128)(2,1)}, bf16[256,2048]{1,0:T(8,128)(2,1)}, f32[1024,2048]{1,0:T(8,128)}) custom-call(bf16[256,2048]{1,0:T(8,128)(2,1)} %acts_ref.1, bf16[1024,2048]{1,0:T(8,128)(2,1)} %wrot_ref.1, bf16[256,2048]{1,0:T(8,128)(2,1)} %up_ref.1, bf16[8,128,128]{2,1,0:T(8,128)(2,1)} %get-tuple-element.10.left_ref, ...), custom_call_target="tpu_custom_call" | custom-call | flops 25769803776 | bytes 33554432 | tf_op jit(solution)/shard_map/pallas_call | solution.py:520
  209.4 0.0 copy-start
  209.4 3.4 %copy-done = f32[1024,2048]{1,0:T(8,128)S(1)} copy-done((f32[1024,2048]{1,0:T(8,128)S(1)}, f32[1024,2048]{1,0:T(8,128)}, u32[]{:S(2)}) %copy-start) | copy-done | bytes 8388632
  212.8 0.0 copy-start.1
  212.8 1.2 copy-done.1
  214.0 0.0 copy-start.2
  214.0 1.2 copy-done.2
  215.3 5.0 %shard_map.68 = (bf16[256,2048]{1,0:T(8,128)(2,1)}, bf16[256,2048]{1,0:T(8,128)(2,1)}, f32[1024,2048]{1,0:T(8,128)}) custom-call(bf16[256,2048]{1,0:T(8,128)(2,1)S(1)} %copy-done.1, bf16[256,2048]{1,0:T(8,128)(2,1)S(1)} %copy-done.2, f32[1024,2048]{1,0:T(8,128)S(1)} %copy-done), custom_call_target="tpu_custom_call" | custom-call | tf_op jit(solution)/shard_map/pallas_call | solution.py:494
Async XLA Ops:
  209.4 3.4 %copy-start = (f32[1024,2048]{1,0:T(8,128)S(1)}, f32[1024,2048]{1,0:T(8,128)}, u32[]{:S(2)}) copy-start(f32[1024,2048]{1,0:T(8,128)} %get-tuple-element.8.refs_2_) | copy-start | bytes 25165828
  212.8 1.2 copy-start.1
  214.0 1.2 copy-start.2

commit v5 on v2

--- a/solution.py
+++ b/solution.py
@@ -141,7 +141,14 @@
 
     d1 = remote(acts_ref, x.at[p], d1_send, d1_recv.at[p], dev(z, c, z))
 
-    @pl.when(home == 0)
+    home_column, home_line = lax.rem(z, 2), lax.div(z, 2)
+    home_r = home_column * (n - 1 - home_line) + (1 - home_column) * home_line
+    away = lax.rem(s * (r - home_r) + 2 * n, n)
+    past = lax.div(away + half - 1, n)
+    arc = past * (n - away) + (1 - past) * away
+    turn = 2 * (half - arc) + past + lax.div(arc, half)
+
+    @pl.when(jnp.logical_and(home == 0, turn == 1))
     def _():
         d1.start()
 
@@ -165,21 +172,8 @@
         pltpu.make_async_copy(u.at[u_rows(index)], u.at[u_rows(index)], u_recv.at[index]).wait()
 
     e_copy_long(1).start()
-    e_copy_short(1).start()
-
-    load_w.wait()
     own_rows = pl.ds(pl.multiple_of(c * rows, rows), rows)
-
-    @pl.loop(0, rows // HBLK)
-    def _(b):
-        at = pl.ds(pl.multiple_of(b * HBLK, HBLK), HBLK)
-        to = pl.ds(pl.multiple_of(c * rows + b * HBLK, HBLK), HBLK)
-        mixed = jnp.dot(left_ref[b], w_raw[at, :], preferred_element_type=jnp.float32)
-        w[to, :] = (mixed * (1.0 / HBLK)).astype(jnp.bfloat16)
-
     w_copy = remote(w.at[own_rows], w.at[own_rows], w_sem.at[0], w_sem.at[1], sibling)
-    w_copy.start()
-    e_copy_sib(p).start()
 
     def x_chip(i):
         moved = lax.div(i + n - 1, n) * (half - lax.div(i, 2)) * (1 - 2 * lax.rem(i, 2))
@@ -224,123 +218,175 @@
                                      preferred_element_type=jnp.float32)
             rot[b * HBLK:(b + 1) * HBLK, at] = (turned * (1.0 / HBLK)).astype(jnp.bfloat16)
 
+    def rotate_own(q):
+        rotate(q, 2 * q + c, lambda b: x[
+            q, :, pl.ds(pl.multiple_of(c * rows + b * HBLK, HBLK), HBLK)])
+
+    def out_tile(q, tile):
+        at = pl.ds(pl.multiple_of(tile * tile_cols, tile_cols), tile_cols)
+        po[q, :, at] = jnp.dot(
+            x[q], w[:, at], preferred_element_type=jnp.float32).astype(jnp.bfloat16)
+
     def add_into(total, piece):
         return (total.astype(jnp.float32) + piece.astype(jnp.float32)).astype(jnp.bfloat16)
 
-    c_start = 2
+    c_start = 3
+    tile_cols = cols // SUB
     slots = c_start + n - 1 + pieces
 
     @pl.loop(0, slots)
     def _(t):
-        @pl.when(t == c_start)
+        j = t - dist
+        i, sub = lax.div(j + SUB, SUB) - 1, lax.rem(j + SUB, SUB)
+        here = jnp.logical_and(j >= 0, j < pieces)
+
+        @pl.when(here)
+        def _():
+            q = x_chip(i)
+
+            @pl.when(jnp.logical_and(home == 1, j == 0))
+            def _():
+                load_x.wait()
+
+            @pl.when(jnp.logical_and(home == 1, jnp.logical_and(sub == 0, j > 0)))
+            def _():
+                pltpu.make_async_copy(x.at[q], x.at[q], d1_recv.at[q]).wait()
+
+            @pl.when(home == 0)
+            def _():
+                pltpu.make_async_copy(x.at[q, part(sub)], x.at[q, part(sub)],
+                                      x_recv.at[q * SUB + sub]).wait()
+
+            @pl.when(goes_up)
+            def _():
+                x_copy(q, sub, 0, z + 1).start()
+
+            @pl.when(goes_down)
+            def _():
+                x_copy(q, sub, 1, z - 1).start()
+
+            @pl.when(sub == SUB - 1)
+            def _():
+                xo_copy(q).start()
+
+        jc = t - c_start - c_lag
+
+        @pl.when(jnp.logical_and(jc >= 0, jc < pieces))
+        def _():
+            sub_c = lax.rem(jc, SUB)
+            q = c_chip(lax.div(jc, SUB))
+            at = part(sub_c)
+
+            @pl.when(from_below)
+            def _():
+                pltpu.make_async_copy(below.at[q, at], below.at[q, at],
+                                      c_recv.at[0, q * SUB + sub_c]).wait()
+                pi[q, at, :] = add_into(pi[q, at, :], below[q, at, :])
+
+            @pl.when(from_above)
+            def _():
+                pltpu.make_async_copy(above.at[q, at], above.at[q, at],
+                                      c_recv.at[1, q * SUB + sub_c]).wait()
+                pi[q, at, :] = add_into(pi[q, at, :], above[q, at, :])
+
+            @pl.when(z < p)
+            def _():
+                c_copy_up(q, sub_c).start()
+
+            @pl.when(z > p)
+            def _():
+                c_copy_down(q, sub_c).start()
+
+            @pl.when(jnp.logical_and(home == 1, q == p))
+            def _():
+                ig_ref[at, :] = pi[q, at, :]
+
+            @pl.when(jnp.logical_and(home == 1, q != p))
+            def _():
+                f_copy(q, sub_c).start()
+
+        @pl.when(t == 0)
+        def _():
+            load_w.wait()
+
+            @pl.loop(0, rows // HBLK)
+            def _(b):
+                at = pl.ds(pl.multiple_of(b * HBLK, HBLK), HBLK)
+                to = pl.ds(pl.multiple_of(c * rows + b * HBLK, HBLK), HBLK)
+                mixed = jnp.dot(left_ref[b], w_raw[at, :], preferred_element_type=jnp.float32)
+                w[to, :] = (mixed * (1.0 / HBLK)).astype(jnp.bfloat16)
+
+            w_copy.start()
+            e_copy_sib(p).start()
+
+        @pl.when(jnp.logical_and(t == SUB * turn - 5, jnp.logical_and(home == 0, turn > 1)))
+        def _():
+            d1.start()
+
+        @pl.when(t == 2)
+        def _():
+            e_copy_short(1).start()
+
+        @pl.when(t == c_start - 1)
         def _():
             w_copy.wait_recv()
 
         for step in range(1, half + 1):
-            @pl.when(t == SUB * step)
+            @pl.when(t == SUB * (2 * step - 1) + c_start - 1)
             def _(step=step):
-                first = ring(-s * step)
-                u_arrived(2 * first + c)
+                source = ring(-s * step)
+                u_arrived(2 * source + c)
                 if step < half:
                     e_copy_long(step + 1).start()
-                e_copy_sib(first).start()
-                if step < half:
-                    second = ring(s * step)
-                    u_arrived(2 * second + c)
-                    if step < half - 1:
-                        e_copy_short(step + 1).start()
-                    e_copy_sib(second).start()
-
-        j = t - dist
-
-        @pl.when(jnp.logical_and(j >= 0, j < pieces))
-        def _():
-            i, sub = lax.div(j, SUB), lax.rem(j, SUB)
-            q = x_chip(i)
-
-            @pl.when(jnp.logical_and(home == 1, j == 0))
-            def _():
-                load_x.wait()
-
-            @pl.when(jnp.logical_and(home == 1, jnp.logical_and(sub == 0, j > 0)))
-            def _():
-                pltpu.make_async_copy(x.at[q], x.at[q], d1_recv.at[q]).wait()
-
-            @pl.when(home == 0)
-            def _():
-                pltpu.make_async_copy(x.at[q, part(sub)], x.at[q, part(sub)],
-                                      x_recv.at[q * SUB + sub]).wait()
-
-            @pl.when(goes_up)
-            def _():
-                x_copy(q, sub, 0, z + 1).start()
-
-            @pl.when(goes_down)
-            def _():
-                x_copy(q, sub, 1, z - 1).start()
-
-            @pl.when(sub == SUB - 1)
-            def _():
-                xo_copy(q).start()
-
-                @pl.loop(0, cols // TILE)
+                e_copy_sib(source).start()
+
+        for step in range(1, half):
+            @pl.when(t == 2 * SUB * step + c_start - 1)
+            def _(step=step):
+                source = ring(s * step)
+                u_arrived(2 * source + c)
+                if step < half - 1:
+                    e_copy_short(step + 1).start()
+                e_copy_sib(source).start()
+
+        jn = jc + 1
+
+        @pl.when(jnp.logical_and(jnp.logical_and(jn >= 0, jn < pieces),
+                                 lax.rem(jn + slots * SUB, SUB) == 0))
+        def _():
+            q = c_chip(lax.div(jn, SUB))
+
+            @pl.loop(0, feats // TILE)
+            def _(tile):
+                cut = pl.ds(pl.multiple_of(tile * TILE, TILE), TILE)
+                pi[q, :, cut] = lax.dot_general(
+                    u[u_rows(2 * q + c), :], w[cut, :], (((1,), (1,)), ((), ())),
+                    preferred_element_type=jnp.float32).astype(jnp.bfloat16)
+
+        @pl.when(here)
+        def _():
+            @pl.when(jnp.logical_and(i > 0, sub < 2))
+            def _():
+                done = x_chip(i - 1)
+                for tile in range(SUB // 2):
+                    out_tile(done, sub * (SUB // 2) + tile)
+
+            @pl.when(jnp.logical_and(i > 0, sub == 2))
+            def _():
+                rotate_own(x_chip(i - 1))
+
+            @pl.when(j == pieces - 1)
+            def _():
+                q = x_chip(n - 1)
+
+                @pl.loop(0, SUB)
                 def _(tile):
-                    at = pl.ds(pl.multiple_of(tile * TILE, TILE), TILE)
-                    po[q, :, at] = jnp.dot(
-                        x[q], w[:, at], preferred_element_type=jnp.float32).astype(jnp.bfloat16)
-
-                rotate(q, 2 * q + c, lambda b: x[
-                    q, :, pl.ds(pl.multiple_of(c * rows + b * HBLK, HBLK), HBLK)])
-
-        jc = t - c_start - c_lag
-
-        @pl.when(jnp.logical_and(jc >= 0, jc < pieces))
-        def _():
-            i, sub = lax.div(jc, SUB), lax.rem(jc, SUB)
-            q = c_chip(i)
-            at = part(sub)
-
-            @pl.when(sub == 0)
-            def _():
-                @pl.loop(0, feats // TILE)
-                def _(tile):
-                    cut = pl.ds(pl.multiple_of(tile * TILE, TILE), TILE)
-                    pi[q, :, cut] = lax.dot_general(
-                        u[u_rows(2 * q + c), :], w[cut, :], (((1,), (1,)), ((), ())),
-                        preferred_element_type=jnp.float32).astype(jnp.bfloat16)
-
-            @pl.when(from_below)
-            def _():
-                pltpu.make_async_copy(below.at[q, at], below.at[q, at],
-                                      c_recv.at[0, q * SUB + sub]).wait()
-                pi[q, at, :] = add_into(pi[q, at, :], below[q, at, :])
-
-            @pl.when(from_above)
-            def _():
-                pltpu.make_async_copy(above.at[q, at], above.at[q, at],
-                                      c_recv.at[1, q * SUB + sub]).wait()
-                pi[q, at, :] = add_into(pi[q, at, :], above[q, at, :])
-
-            @pl.when(z < p)
-            def _():
-                c_copy_up(q, sub).start()
-
-            @pl.when(z > p)
-            def _():
-                c_copy_down(q, sub).start()
-
-            @pl.when(jnp.logical_and(home == 1, q == p))
-            def _():
-                ig_ref[at, :] = pi[q, at, :]
-
-            @pl.when(jnp.logical_and(home == 1, q != p))
-            def _():
-                f_copy(q, sub).start()
+                    out_tile(q, tile)
 
         for k in range(half, 0, -1):
             i = 1 if k == half else 2 * (half - k)
 
-            @pl.when(t == n - 1 + SUB * i + SUB - 1)
+            @pl.when(t == n - 1 + SUB * i + SUB + 1)
             def _(k=k):
                 if k < half:
                     rl_copy(k + 1).wait_recv()
@@ -349,13 +395,15 @@
                 rl_copy(k).start()
 
         for k in range(half - 1, 0, -1):
-            @pl.when(t == n - 1 + SUB * (2 * (half - k) + 1) + SUB - 1)
+            @pl.when(t == n - 1 + SUB * (2 * (half - k) + 1) + SUB - 1 + 2 * min(k - 1, 1))
             def _(k=k):
                 if k < half - 1:
                     rr_copy(k + 1).wait_recv()
                     q = ring(-s * k)
                     po[q] = add_into(po[q], rs_short[k])
                 rr_copy(k).start()
+
+    rotate_own(x_chip(n - 1))
 
     @pl.loop(0, n)
     def _(q):
@@ -428,6 +476,26 @@
             @pl.when(jnp.logical_and(home == 1, q != p))
             def _():
                 f_copy(q, sub).wait_send()
+
+
+COPY_PARTS = 8
+
+
+def copy_kernel(*refs):
+    for source, target in zip(refs[:3], refs[3:]):
+        target[...] = source[...]
+
+
+def hand_on(arrays):
+    specs = [pl.BlockSpec((a.shape[0] // COPY_PARTS, a.shape[1]), lambda i: (i, 0)) for a in arrays]
+    return pl.pallas_call(
+        copy_kernel,
+        grid=(COPY_PARTS,),
+        out_shape=tuple(jax.ShapeDtypeStruct(a.shape, a.dtype) for a in arrays),
+        in_specs=specs,
+        out_specs=tuple(specs),
+        compiler_params=pltpu.CompilerParams(vmem_limit_bytes=60 << 20),
+    )(*arrays)
 
 
 def fused(acts, w_rot, signs, upstream):
@@ -446,7 +514,7 @@
     vmem = pl.BlockSpec(memory_space=pltpu.VMEM)
     hbm = pl.BlockSpec(memory_space=pl.ANY)
     tokens = 2 * n * tok
-    return pl.pallas_call(
+    return hand_on(pl.pallas_call(
         functools.partial(kernel, n),
         out_shape=(
             jax.ShapeDtypeStruct((tok, cols), bf),
@@ -478,7 +546,7 @@
             collective_id=0, has_side_effects=True, vmem_limit_bytes=60 << 20),
         cost_estimate=pl.CostEstimate(
             flops=6 * tokens * rows * cols, bytes_accessed=16 * rows * cols, transcendentals=0),
-    )(acts, w_rot, upstream, left, right)
+    )(acts, w_rot, upstream, left, right))
 
 
 def solution(mesh):

time: 215 us -> 185 us (0.86); the launches traced: 214 us -> 182 us
  Pallas kernels: 200 us -> 179 us
  local copies, waits for them, and re-layouts: 12.5 us -> 0 us
    pallas_call x1, Pallas kernels: 200 us -> 169 us  [fused(): pl.pallas_call(functools.partial(kernel, n), out_shape=(jax.ShapeDtypeStr...]
    unnamed x3 -> x0, local copies, waits for them, and re-layouts: 12.5 us -> none
    pallas_call x0 -> x1, Pallas kernels: none -> 10.2 us  [hand_on(): pl.pallas_call(copy_kernel, grid=(COPY_PARTS,), out_shape=tuple((jax.Shap...]
where the time goes in v5:
time: 185 us; the launch traced here: 182 us
  Pallas kernels  179 us (97%)
    pallas_call x1, Pallas kernels, fused(): pl.pallas_call(functools.partial(kernel, n), out_shape=(jax.ShapeDtypeStr...  169 us
    pallas_call x1, Pallas kernels, hand_on(): pl.pallas_call(copy_kernel, grid=(COPY_PARTS,), out_shape=tuple((jax.Shap...  10.2 us

profile of v5, /device:TPU:0, one launch (start us, length us, event | category | flops | bytes accessed | tf_op | source)
XLA Modules:
  0.0 181.8 jit_solution(13747147075054724341)
XLA Ops:
  0.6 0.7 convert_bitcast_fusion
  1.3 0.1 subtract_convert_fusion
  1.4 1.0 multiply_convert_fusion
  2.4 169.2 %shard_map.67 = (bf16[256,2048]{1,0:T(8,128)(2,1)}, bf16[256,2048]{1,0:T(8,128)(2,1)}, f32[1024,2048]{1,0:T(8,128)}) custom-call(bf16[256,2048]{1,0:T(8,128)(2,1)} %acts_ref.1, bf16[1024,2048]{1,0:T(8,128)(2,1)} %wrot_ref.1, bf16[256,2048]{1,0:T(8,128)(2,1)} %up_ref.1, bf16[8,128,128]{2,1,0:T(8,128)(2,1)} %get-tuple-element.10.left_ref, ...), custom_call_target="tpu_custom_call" | custom-call | flops 25769803776 | bytes 33554432 | tf_op jit(solution)/shard_map/pallas_call | solution.py:517
  171.6 10.2 %shard_map.68 = (bf16[256,2048]{1,0:T(8,128)(2,1)}, bf16[256,2048]{1,0:T(8,128)(2,1)}, f32[1024,2048]{1,0:T(8,128)}) custom-call(bf16[256,2048]{1,0:T(8,128)(2,1)} %get-tuple-element.6.refs_0_, bf16[256,2048]{1,0:T(8,128)(2,1)} %get-tuple-element.7.refs_1_, f32[1024,2048]{1,0:T(8,128)} %get-tuple-element.8.refs_2_), custom_call_target="tpu_custom_call" | custom-call | tf_op jit(solution)/shard_map/pallas_call | solution.py:491

commit v6 on v5

--- a/solution.py
+++ b/solution.py
@@ -64,7 +64,7 @@
 
 def kernel(n, acts_ref, wrot_ref, up_ref, left_ref, right_ref,
            out_ref, ig_ref, grad_ref,
-           w_raw, w, x, xo, rot, u, pi, below, above, po, rs_long, rs_short, gt,
+           w, x, xo, rot, u, pi, below, above, po, rs_long, rs_short, g,
            load_sem, d1_send, d1_recv, x_send, x_recv, xo_send, xo_recv,
            e_long, e_short, e_sib, u_recv, w_sem, c_send, c_recv, f_send, f_recv,
            rl_send, rl_recv, rr_send, rr_recv, g_sem):
@@ -127,11 +127,13 @@
     def _():
         pl.semaphore_signal(barrier, inc=1, device_id=dev(p, c, z + 1), device_id_type=MESH)
 
-    load_w = pltpu.make_async_copy(wrot_ref, w_raw, load_sem.at[0])
-    load_w.start()
-    load_u = pltpu.make_async_copy(up_ref, u.at[u_rows(l)], load_sem.at[1])
+    load_u = pltpu.make_async_copy(up_ref, u.at[u_rows(l)], load_sem.at[0])
     load_u.start()
-    load_x = pltpu.make_async_copy(acts_ref, x.at[p], load_sem.at[2])
+    load_x = pltpu.make_async_copy(acts_ref, x.at[p], load_sem.at[1])
+    loads_w = [pltpu.make_async_copy(wrot_ref.at[pl.ds(k * tok, tok)], po.at[k], load_sem.at[2 + k])
+               for k in range(rows // tok)]
+    for load in loads_w:
+        load.start()
 
     @pl.when(home == 1)
     def _():
@@ -230,9 +232,22 @@
     def add_into(total, piece):
         return (total.astype(jnp.float32) + piece.astype(jnp.float32)).astype(jnp.bfloat16)
 
-    c_start = 3
+    c_start = 2
     tile_cols = cols // SUB
     slots = c_start + n - 1 + pieces
+    tiles = cols // GRAD_TILE
+
+    def rotate_other(q):
+        pltpu.make_async_copy(xo.at[q], xo.at[q], xo_recv.at[q]).wait()
+        u_arrived(2 * q + 1 - c)
+        rotate(q, 2 * q + 1 - c, lambda b: xo[q, :, b * HBLK:(b + 1) * HBLK])
+
+    def grad_part(q, at):
+        both = pl.ds(pl.multiple_of(2 * q * tok, 2 * tok), 2 * tok)
+        return jnp.dot(rot[:, both], u[both, at], preferred_element_type=jnp.float32)
+
+    def grad_cols(tile):
+        return pl.ds(pl.multiple_of(tile * GRAD_TILE, GRAD_TILE), GRAD_TILE)
 
     @pl.loop(0, slots)
     def _(t):
@@ -307,13 +322,16 @@
 
         @pl.when(t == 0)
         def _():
-            load_w.wait()
+            for load in loads_w:
+                load.wait()
 
             @pl.loop(0, rows // HBLK)
             def _(b):
-                at = pl.ds(pl.multiple_of(b * HBLK, HBLK), HBLK)
+                held = tok // HBLK
+                at = pl.ds(pl.multiple_of(lax.rem(b, held) * HBLK, HBLK), HBLK)
                 to = pl.ds(pl.multiple_of(c * rows + b * HBLK, HBLK), HBLK)
-                mixed = jnp.dot(left_ref[b], w_raw[at, :], preferred_element_type=jnp.float32)
+                mixed = jnp.dot(
+                    left_ref[b], po[lax.div(b, held), at, :], preferred_element_type=jnp.float32)
                 w[to, :] = (mixed * (1.0 / HBLK)).astype(jnp.bfloat16)
 
             w_copy.start()
@@ -383,6 +401,25 @@
                 def _(tile):
                     out_tile(q, tile)
 
+        @pl.when(t == n - 1 + SUB + 3)
+        def _():
+            rotate_other(p)
+
+            @pl.loop(0, tiles)
+            def _(tile):
+                at = grad_cols(tile)
+                g[:, at] = grad_part(p, at)
+
+        @pl.when(t == n - 1 + SUB * (n - 1) + 2)
+        def _():
+            across = ring(half)
+            rotate_other(across)
+
+            @pl.loop(0, tiles)
+            def _(tile):
+                at = grad_cols(tile)
+                g[:, at] += grad_part(across, at)
+
         for k in range(half, 0, -1):
             i = 1 if k == half else 2 * (half - k)
 
@@ -404,30 +441,22 @@
                 rr_copy(k).start()
 
     rotate_own(x_chip(n - 1))
-
-    @pl.loop(0, n)
-    def _(q):
-        pltpu.make_async_copy(xo.at[q], xo.at[q], xo_recv.at[q]).wait()
-        u_arrived(2 * q + 1 - c)
-        rotate(q, 2 * q + 1 - c, lambda b: xo[q, :, b * HBLK:(b + 1) * HBLK])
-
-    def g_copy(tile, slot):
-        at = pl.ds(pl.multiple_of(tile * GRAD_TILE, GRAD_TILE), GRAD_TILE)
-        return pltpu.make_async_copy(gt.at[slot], grad_ref.at[:, at], g_sem.at[slot])
-
-    tiles = cols // GRAD_TILE
+    others = [ring(way * k) for k in range(1, half) for way in (1, -1)]
+    for q in others:
+        rotate_other(q)
+
+    def g_copy(tile):
+        at = grad_cols(tile)
+        return pltpu.make_async_copy(g.at[:, at], grad_ref.at[:, at], g_sem.at[tile])
 
     @pl.loop(0, tiles)
     def _(tile):
-        slot = lax.rem(tile, 2)
-
-        @pl.when(tile >= 2)
-        def _():
-            g_copy(tile - 2, slot).wait()
-
-        at = pl.ds(pl.multiple_of(tile * GRAD_TILE, GRAD_TILE), GRAD_TILE)
-        gt[slot] = jnp.dot(rot[...], u[:, at], preferred_element_type=jnp.float32)
-        g_copy(tile, slot).start()
+        at = grad_cols(tile)
+        total = g[:, at]
+        for q in others:
+            total += grad_part(q, at)
+        g[:, at] = total
+        g_copy(tile).start()
 
     rl_copy(1).wait_recv()
     rr_copy(1).wait_recv()
@@ -440,8 +469,8 @@
             pltpu.make_async_copy(ig_ref.at[part(sub)], ig_ref.at[part(sub)], f_recv.at[sub]).wait()
         d1.wait_send()
 
-    for tile in (tiles - 2, tiles - 1):
-        g_copy(tile, tile % 2).wait()
+    for tile in range(tiles):
+        g_copy(tile).wait()
     w_copy.wait_send()
     for step in range(1, half + 1):
         e_copy_long(step).wait_send()
@@ -481,19 +510,35 @@
 COPY_PARTS = 8
 
 
-def copy_kernel(*refs):
-    for source, target in zip(refs[:3], refs[3:]):
-        target[...] = source[...]
+def copy_kernel(out_ref, ig_ref, grad_ref, out_to, ig_to, grad_to,
+                out_buf, ig_buf, grad_buf, load_sems, store_sems):
+    rows = grad_ref.shape[0] // COPY_PARTS
+    moves = [(out_ref, out_buf, out_to), (ig_ref, ig_buf, ig_to)]
+    for part in range(COPY_PARTS):
+        at = pl.ds(part * rows, rows)
+        moves.append((grad_ref.at[at], grad_buf.at[at], grad_to.at[at]))
+    loads = [pltpu.make_async_copy(source, held, load_sems.at[k])
+             for k, (source, held, target) in enumerate(moves)]
+    stores = [pltpu.make_async_copy(held, target, store_sems.at[k])
+              for k, (source, held, target) in enumerate(moves)]
+    for load in loads:
+        load.start()
+    for load, store in zip(loads, stores):
+        load.wait()
+        store.start()
+    for store in stores:
+        store.wait()
 
 
 def hand_on(arrays):
-    specs = [pl.BlockSpec((a.shape[0] // COPY_PARTS, a.shape[1]), lambda i: (i, 0)) for a in arrays]
+    hbm = pl.BlockSpec(memory_space=pl.ANY)
     return pl.pallas_call(
         copy_kernel,
-        grid=(COPY_PARTS,),
         out_shape=tuple(jax.ShapeDtypeStruct(a.shape, a.dtype) for a in arrays),
-        in_specs=specs,
-        out_specs=tuple(specs),
+        in_specs=[hbm] * 3,
+        out_specs=(hbm,) * 3,
+        scratch_shapes=[pltpu.VMEM(a.shape, a.dtype) for a in arrays]
+        + [pltpu.SemaphoreType.DMA((2 + COPY_PARTS,))] * 2,
         compiler_params=pltpu.CompilerParams(vmem_limit_bytes=60 << 20),
     )(*arrays)
 
@@ -524,7 +569,6 @@
         in_specs=[hbm, hbm, hbm, vmem, vmem],
         out_specs=(vmem, vmem, hbm),
         scratch_shapes=[
-            pltpu.VMEM((rows, cols), bf),
             pltpu.VMEM((feats, cols), bf),
             pltpu.VMEM((n, tok, feats), bf),
             pltpu.VMEM((n, tok, rows), bf),
@@ -536,11 +580,11 @@
             pltpu.VMEM((n, tok, cols), bf),
             pltpu.VMEM((half, tok, cols), bf),
             pltpu.VMEM((half - 1, tok, cols), bf),
-            pltpu.VMEM((2, rows, GRAD_TILE), jnp.float32),
-            dma((3,)), dma, dma((n,)), dma((2, n * SUB)), dma((n * SUB,)), dma((n,)), dma((n,)),
+            pltpu.VMEM((rows, cols), jnp.float32),
+            dma((2 + rows // tok,)), dma, dma((n,)), dma((2, n * SUB)), dma((n * SUB,)), dma((n,)), dma((n,)),
             dma((half,)), dma((half - 1,)), dma((n,)), dma((2 * n,)), dma((2,)),
             dma((n * SUB,)), dma((2, n * SUB)), dma((n * SUB,)), dma((SUB,)),
-            dma((half,)), dma((half,)), dma((half - 1,)), dma((half - 1,)), dma((2,)),
+            dma((half,)), dma((half,)), dma((half - 1,)), dma((half - 1,)), dma((cols // GRAD_TILE,)),
         ],
         compiler_params=pltpu.CompilerParams(
             collective_id=0, has_side_effects=True, vmem_limit_bytes=60 << 20),

time: 185 us -> 181 us (0.978)
  Pallas kernels: 179 us -> 175 us
    pallas_call x1, Pallas kernels: 169 us -> 167 us  [fused(): pl.pallas_call(functools.partial(kernel, n), out_shape=(jax.ShapeDtypeStr...]
    pallas_call x1, Pallas kernels: 10.2 us -> 8.19 us  [hand_on(): pl.pallas_call(copy_kernel, out_shape=tuple((jax.ShapeDtypeStruct(a.shape...]
where the time goes in v6:
time: 181 us; the launch traced here: 177 us
  Pallas kernels  175 us (97%)
    pallas_call x1, Pallas kernels, fused(): pl.pallas_call(functools.partial(kernel, n), out_shape=(jax.ShapeDtypeStr...  167 us
    pallas_call x1, Pallas kernels, hand_on(): pl.pallas_call(copy_kernel, out_shape=tuple((jax.ShapeDtypeStruct(a.shape...  8.19 us

profile of v6, /device:TPU:0, one launch (start us, length us, event | category | flops | bytes accessed | tf_op | source)
XLA Modules:
  0.0 177.4 jit_solution(162569533518040730)
XLA Ops:
  0.6 0.7 convert_bitcast_fusion
  1.3 0.1 subtract_convert_fusion
  1.4 1.0 multiply_convert_fusion
  2.4 166.8 %shard_map.67 = (bf16[256,2048]{1,0:T(8,128)(2,1)}, bf16[256,2048]{1,0:T(8,128)(2,1)}, f32[1024,2048]{1,0:T(8,128)}) custom-call(bf16[256,2048]{1,0:T(8,128)(2,1)} %acts_ref.1, bf16[1024,2048]{1,0:T(8,128)(2,1)} %wrot_ref.1, bf16[256,2048]{1,0:T(8,128)(2,1)} %up_ref.1, bf16[8,128,128]{2,1,0:T(8,128)(2,1)} %get-tuple-element.10.left_ref, ...), custom_call_target="tpu_custom_call" | custom-call | flops 25769803776 | bytes 33554432 | tf_op jit(solution)/shard_map/pallas_call | solution.py:562
  169.2 8.2 %shard_map.68 = (bf16[256,2048]{1,0:T(8,128)(2,1)}, bf16[256,2048]{1,0:T(8,128)(2,1)}, f32[1024,2048]{1,0:T(8,128)}) custom-call(bf16[256,2048]{1,0:T(8,128)(2,1)} %get-tuple-element.6.out_ref, bf16[256,2048]{1,0:T(8,128)(2,1)} %get-tuple-element.7.ig_ref, f32[1024,2048]{1,0:T(8,128)} %get-tuple-element.8.grad_ref), custom_call_target="tpu_custom_call" | custom-call | tf_op jit(solution)/shard_map/pallas_call | solution.py:535

commit v7 on v6

--- a/solution.py
+++ b/solution.py
@@ -56,7 +56,7 @@
     return outputs, input_grad, grad_rot
 
 
-SUB = 4
+SUB = 8
 TILE = 512
 GRAD_TILE = 256
 MESH = pl.DeviceIdType.MESH
@@ -232,7 +232,7 @@
     def add_into(total, piece):
         return (total.astype(jnp.float32) + piece.astype(jnp.float32)).astype(jnp.bfloat16)
 
-    c_start = 2
+    c_start = 4
     tile_cols = cols // SUB
     slots = c_start + n - 1 + pieces
     tiles = cols // GRAD_TILE
@@ -337,11 +337,11 @@
             w_copy.start()
             e_copy_sib(p).start()
 
-        @pl.when(jnp.logical_and(t == SUB * turn - 5, jnp.logical_and(home == 0, turn > 1)))
+        @pl.when(jnp.logical_and(t == SUB * turn - 12, jnp.logical_and(home == 0, turn > 1)))
         def _():
             d1.start()
 
-        @pl.when(t == 2)
+        @pl.when(t == 3)
         def _():
             e_copy_short(1).start()
 

time: 181 us -> 197 us (1.088)
  the two profiles are of different devices: /device:TPU:0 before, /device:TPU:24 now
where the time goes in v7:
time: 197 us
  Pallas kernels  195 us (99%)
    pallas_call x1, Pallas kernels, fused(): pl.pallas_call(functools.partial(kernel, n), out_shape=(jax.ShapeDtypeStr...  186 us
    pallas_call x1, Pallas kernels, hand_on(): pl.pallas_call(copy_kernel, out_shape=tuple((jax.ShapeDtypeStruct(a.shape...  8.19 us

profile of v7, /device:TPU:24, one launch (start us, length us, event | category | flops | bytes accessed | tf_op | source)
XLA Modules:
  0.0 197.0 jit_solution(14522420150297301201)
XLA Ops:
  0.6 0.7 convert_bitcast_fusion
  1.3 0.1 subtract_convert_fusion
  1.4 1.0 multiply_convert_fusion
  2.4 186.4 %shard_map.67 = (bf16[256,2048]{1,0:T(8,128)(2,1)}, bf16[256,2048]{1,0:T(8,128)(2,1)}, f32[1024,2048]{1,0:T(8,128)}) custom-call(bf16[256,2048]{1,0:T(8,128)(2,1)} %acts_ref.1, bf16[1024,2048]{1,0:T(8,128)(2,1)} %wrot_ref.1, bf16[256,2048]{1,0:T(8,128)(2,1)} %up_ref.1, bf16[8,128,128]{2,1,0:T(8,128)(2,1)} %get-tuple-element.10.left_ref, ...), custom_call_target="tpu_custom_call" | custom-call | flops 25769803776 | bytes 33554432 | tf_op jit(solution)/shard_map/pallas_call | solution.py:562
  188.8 8.2 %shard_map.68 = (bf16[256,2048]{1,0:T(8,128)(2,1)}, bf16[256,2048]{1,0:T(8,128)(2,1)}, f32[1024,2048]{1,0:T(8,128)}) custom-call(bf16[256,2048]{1,0:T(8,128)(2,1)} %get-tuple-element.6.out_ref, bf16[256,2048]{1,0:T(8,128)(2,1)} %get-tuple-element.7.ig_ref, f32[1024,2048]{1,0:T(8,128)} %get-tuple-element.8.grad_ref), custom_call_target="tpu_custom_call" | custom-call | tf_op jit(solution)/shard_map/pallas_call | solution.py:535

commit v8 on v6

--- a/solution.py
+++ b/solution.py
@@ -337,7 +337,7 @@
             w_copy.start()
             e_copy_sib(p).start()
 
-        @pl.when(jnp.logical_and(t == SUB * turn - 5, jnp.logical_and(home == 0, turn > 1)))
+        @pl.when(jnp.logical_and(t == SUB * turn - 8, jnp.logical_and(home == 0, turn > 1)))
         def _():
             d1.start()
 

time: 181 us -> 178 us (0.983); the launches traced: 177 us -> 177 us
  no operation moved by 1% of the time
where the time goes in v8:
time: 178 us; the launch traced here: 177 us
  Pallas kernels  174 us (98%)
    pallas_call x1, Pallas kernels, fused(): pl.pallas_call(functools.partial(kernel, n), out_shape=(jax.ShapeDtypeStr...  166 us
    pallas_call x1, Pallas kernels, hand_on(): pl.pallas_call(copy_kernel, out_shape=tuple((jax.ShapeDtypeStruct(a.shape...  8.19 us

profile of v8, /device:TPU:0, one launch (start us, length us, event | category | flops | bytes accessed | tf_op | source)
XLA Modules:
  0.0 176.8 jit_solution(659927763500333797)
XLA Ops:
  0.6 0.7 convert_bitcast_fusion
  1.3 0.1 subtract_convert_fusion
  1.4 1.0 multiply_convert_fusion
  2.4 166.2 %shard_map.67 = (bf16[256,2048]{1,0:T(8,128)(2,1)}, bf16[256,2048]{1,0:T(8,128)(2,1)}, f32[1024,2048]{1,0:T(8,128)}) custom-call(bf16[256,2048]{1,0:T(8,128)(2,1)} %acts_ref.1, bf16[1024,2048]{1,0:T(8,128)(2,1)} %wrot_ref.1, bf16[256,2048]{1,0:T(8,128)(2,1)} %up_ref.1, bf16[8,128,128]{2,1,0:T(8,128)(2,1)} %get-tuple-element.10.left_ref, ...), custom_call_target="tpu_custom_call" | custom-call | flops 25769803776 | bytes 33554432 | tf_op jit(solution)/shard_map/pallas_call | solution.py:562
  168.6 8.2 %shard_map.68 = (bf16[256,2048]{1,0:T(8,128)(2,1)}, bf16[256,2048]{1,0:T(8,128)(2,1)}, f32[1024,2048]{1,0:T(8,128)}) custom-call(bf16[256,2048]{1,0:T(8,128)(2,1)} %get-tuple-element.6.out_ref, bf16[256,2048]{1,0:T(8,128)(2,1)} %get-tuple-element.7.ig_ref, f32[1024,2048]{1,0:T(8,128)} %get-tuple-element.8.grad_ref), custom_call_target="tpu_custom_call" | custom-call | tf_op jit(solution)/shard_map/pallas_call | solution.py:535
